TPU v7x, 32 devices: a whole 2x2x4 slice. The times are simulated.
32 devices in a mesh: seq: 8 (over z, x), inner: 4 (over y, core).
Axes of the slice: x: 2, y: 2, z: 4, core: 2. Of those that a mesh axis runs over, the one named last changes fastest.
Arguments:
- log_mel: bfloat16 [28672, 320], P(('seq', 'inner')), may hold values from -6 to 6
- lengths: int32 [32, 4], replicated, may hold values from 1 to 893, as said below
- first_kernel: bfloat16 [9, 128], replicated, may hold values from -2 to 2
- first_bias: float32 [128], replicated, may hold values from -3 to 3
- second_kernel: bfloat16 [1152, 128], replicated, may hold values from -0.1875 to 0.1875
- second_bias: float32 [128], replicated, may hold values from -3 to 3
- embed_weight: bfloat16 [2560, 1024], replicated, may hold values from -0.125 to 0.125
- norm_gain: float32 [1024], replicated, may hold values from 0.1 to 1.9
- head_weight: bfloat16 [1024, 3072], replicated
- output_weight: bfloat16 [1024, 1024], replicated, may hold values from -0.1875 to 0.1875
Outputs:
- encoded: bfloat16 [16384, 1024], P(('seq', 'inner'))
Inputs may be any that keep to these rules, and one draw needn't show every extreme that they name: `lengths`: every length is 1 or more. The frames of owner d begin at d * 512 + e_d with e_d between -192 and 192; e_0 = 0, the frames of all owners together are exactly 16384, and in every draw some owner has e_d = 192 and another e_d = -192. In every draw some utterance has exactly 893 frames.
All inputs are finite; a program needn't handle non-finite values.
Results may differ from a plain program's by a relative error of at most 0.008.
The roundings to bfloat16 on the way count: a program that leaves them out, or rounds other values in their place, can miss the bound.
Values may be sent and summed in bfloat16 or wider, within the bound.
No kernel may reach another device: no remote copies, remote signals or barrier semaphores. Data moves between devices by JAX's collectives and lax.ppermute only.
A program may use at most 256 MiB of HBM per device.

v0:
```python
import jax
import jax.numpy as jnp
from jax import lax
from jax.experimental import pallas as pl
from jax.experimental.pallas import tpu as pltpu
from jax.sharding import PartitionSpec as P

HEADS = 16
SPAN = 64
LEFT_SPANS = 4
CTX = 320
SHARD = 512
MARGIN = 192
CAP = 896
WIN = CTX + SHARD + SPAN
MEL = 80
CH = 128
PAIRS = MEL // 4
D = 1024
HEAD = D // HEADS
ROWS = 448
QROWS = 128
KROWS = 512
AXES = ("seq", "inner")
F32 = jnp.float32
BF16 = jnp.bfloat16


def iota(shape, dim):
    return lax.broadcasted_iota(jnp.int32, shape, dim)


def frame_facts(me, len_ref):
    lens = len_ref[...].astype(F32)
    utts, devices = lens.shape
    lane = iota((devices, devices), 1)
    sub = iota((devices, devices), 0)
    owner_len = jnp.sum(lens, axis=0, keepdims=True)
    lane_row = iota((1, devices), 1)
    own_low = jnp.sum(jnp.where(lane_row < me, owner_len, 0.0), axis=1, keepdims=True)
    own_high = own_low + jnp.sum(jnp.where(lane_row == me, owner_len, 0.0), axis=1, keepdims=True)
    start = jnp.sum(jnp.where(lane < sub, owner_len, 0.0), axis=1, keepdims=True)
    total = (devices * SHARD) * 1.0
    frame = (iota((1, WIN), 1) + (me * SHARD - CTX)).astype(F32)
    begin = jnp.zeros((1, WIN), F32)
    end = jnp.full((1, WIN), total, F32)
    for u in range(utts):
        reached = start <= frame
        begin = jnp.maximum(begin, jnp.max(jnp.where(reached, start, 0.0), axis=0, keepdims=True))
        end = jnp.minimum(end, jnp.min(jnp.where(reached, total, start), axis=0, keepdims=True))
        start = start + jnp.sum(
            jnp.where(lane == sub, lens[u : u + 1, :], 0.0), axis=1, keepdims=True
        )
    return frame, begin, end, own_low, own_high


def window_taps(frame, begin, own_low, own_high, own_ref, up_ref, down_ref, x_ref):
    low = frame[:, 128:512] >= own_low
    high = frame[:, 640:] < own_high
    win = jnp.concatenate(
        [
            up_ref[:, :128].astype(F32),
            jnp.where(low, own_ref[:, :384].astype(F32), up_ref[:, 128:].astype(F32)),
            own_ref[:, 384:512].astype(F32),
            jnp.where(high, own_ref[:, 512:768].astype(F32), down_ref[...].astype(F32)),
        ],
        axis=1,
    )
    prev = pltpu.roll(win[MEL:], 1, 1)
    fresh = begin == frame
    row = iota((16, WIN), 0)
    ones = jnp.where(row < 3, 1.0, 0.0)
    first = jnp.where((row == 3) & fresh, 1.0, ones)
    head = jnp.where(fresh, 0.0, prev[2 * MEL :])
    x_ref[0] = jnp.concatenate([prev, first], axis=0).T.astype(BF16)
    x_ref[1] = jnp.concatenate([head, win[: 2 * MEL], ones], axis=0).T.astype(BF16)
    x_ref[2] = jnp.concatenate([win[MEL:], ones], axis=0).T.astype(BF16)


def second_weights(k2_ref, w2_ref):
    for tap in range(3):
        base = tap * 3 * CH
        w2_ref[tap, :, :CH] = k2_ref[base + CH : base + 3 * CH, :]
        w2_ref[tap, :CH, CH:] = jnp.zeros((CH, CH), BF16)
        w2_ref[tap, CH:, CH:] = k2_ref[base : base + CH, :]


def first_weights(pair, k1, bias_rows):
    row = iota((3 * MEL, CH), 0)
    frame_row = [(row >= MEL * a) & (row < MEL * (a + 1)) for a in range(3)]
    bin_row = row - jnp.where(row >= 2 * MEL, 2 * MEL, jnp.where(row >= MEL, MEL, 0))
    taps = []
    for b in range(3):
        taps.append(
            jnp.where(
                frame_row[0],
                k1[b : b + 1],
                jnp.where(frame_row[1], k1[3 + b : 4 + b], k1[6 + b : 7 + b]),
            )
        )
    halves = []
    for half in range(2):
        at = bin_row - (2 * (2 * pair + half) - 1)
        value = jnp.where(at == 0, taps[0], jnp.where(at == 1, taps[1], 0.0))
        value = jnp.where(at == 2, taps[2], value)
        halves.append(jnp.concatenate([value, bias_rows], axis=0))
    return jnp.concatenate(halves, axis=1).astype(BF16)


def layer_kernel(
    me_ref, len_ref, own_ref, up_ref, down_ref, k1_ref, b1_ref, k2_ref, b2_ref, gain_ref,
    we_hbm, wh_hbm, wo_hbm, out_ref,
    we_ref, wh_ref, wo_ref, x_ref, w2_ref, sec_ref, low_ref, emb_ref, norm_ref,
    q_ref, k_ref, vt_ref, mask_ref, mixed_ref, sems,
):
    copies = [
        pltpu.make_async_copy(src, dst, sems.at[i])
        for i, (src, dst) in enumerate(((we_hbm, we_ref), (wh_hbm, wh_ref), (wo_hbm, wo_ref)))
    ]
    for copy in copies:
        copy.start()
    frame, begin, end, own_low, own_high = frame_facts(me_ref[0], len_ref)
    window_taps(frame, begin, own_low, own_high, own_ref, up_ref, down_ref, x_ref)
    second_weights(k2_ref, w2_ref)
    low_ref[...] = jnp.zeros_like(low_ref)
    bias = b1_ref[...]
    b_high = bias.astype(BF16).astype(F32)
    b_mid = (bias - b_high).astype(BF16).astype(F32)
    b_low = bias - b_high - b_mid
    row = iota((16, CH), 0)
    bias_rows = jnp.where(row == 0, b_high, jnp.where(row == 1, b_mid, b_low))
    bias_rows = jnp.where(row < 3, bias_rows, jnp.where(row == 3, -1e30, 0.0))
    k1 = k1_ref[...].astype(F32)
    bias_2 = b2_ref[...]

    def conv_pair(pair, carry):
        w1 = first_weights(pair, k1, bias_rows)
        for t in range(WIN // ROWS):
            rows = slice(t * ROWS, (t + 1) * ROWS)
            acc = None
            for tap in range(3):
                h = jnp.dot(x_ref[tap, rows, :], w1, preferred_element_type=F32)
                h = jnp.maximum(h, 0.0).astype(BF16)
                part = jnp.dot(h, w2_ref[tap], preferred_element_type=F32)
                acc = part if acc is None else acc + part
            value = jnp.maximum(acc[:, :CH] + low_ref[rows, :] + bias_2, 0.0).astype(BF16)
            low_ref[rows, :] = acc[:, CH:]
            sec_ref[rows, pl.ds(pl.multiple_of(pair * CH, CH), CH)] = value
        return carry

    lax.fori_loop(0, PAIRS, conv_pair, 0)

    copies[0].wait()
    gain = gain_ref[...]
    for t in range(WIN // ROWS):
        rows = slice(t * ROWS, (t + 1) * ROWS)
        emb = jnp.dot(sec_ref[rows, :], we_ref[...], preferred_element_type=F32).astype(BF16)
        emb_ref[rows, :] = emb
        values = emb.astype(F32)
        center = values - jnp.mean(values, axis=1, keepdims=True)
        spread = jnp.mean(center * center, axis=1, keepdims=True)
        norm_ref[rows, :] = (center * lax.rsqrt(spread + 1e-05) * gain).astype(BF16)

    copies[1].wait()
    q = jnp.dot(norm_ref[CTX : CTX + SHARD, :], wh_ref[:, :D], preferred_element_type=F32)
    q_ref[...] = q.astype(BF16) * (HEAD**-0.5)
    for t in range(WIN // ROWS):
        rows = slice(t * ROWS, (t + 1) * ROWS)
        k = jnp.dot(norm_ref[rows, :], wh_ref[:, D : 2 * D], preferred_element_type=F32)
        k_ref[rows, :] = k.astype(BF16)
    for t in range(WIN // 128):
        rows = slice(t * 128, (t + 1) * 128)
        v = jnp.dot(norm_ref[rows, :], wh_ref[:, 2 * D :], preferred_element_type=F32)
        vt_ref[:, rows] = v.T.astype(BF16)

    query = frame[:, CTX : CTX + SHARD]
    q_begin = begin[:, CTX : CTX + SHARD]
    span_at = jnp.floor((query - q_begin) * (1.0 / SPAN)) * SPAN
    key_low = q_begin + jnp.maximum(span_at - LEFT_SPANS * SPAN, 0.0)
    key_high = jnp.minimum(q_begin + span_at + SPAN, end[:, CTX : CTX + SHARD])
    first_frame = (me_ref[0] * SHARD - CTX).astype(F32)
    for i in range(SHARD // QROWS):
        cols = slice(i * QROWS, (i + 1) * QROWS)
        key = iota((KROWS, QROWS), 0).astype(F32) + (first_frame + i * QROWS)
        seen = (key >= key_low[:, cols]) & (key < key_high[:, cols])
        mask_ref[:, cols] = jnp.where(seen, 0.0, -jnp.inf)

    lane = iota((QROWS, 2 * HEAD), 1)

    def attend_tile(step, carry):
        i = step // (HEADS // 2)
        pair = step % (HEADS // 2)
        q_at = pl.multiple_of(i * QROWS, QROWS)
        col = pl.multiple_of(pair * 2 * HEAD, 2 * HEAD)
        keys = k_ref[pl.ds(q_at, KROWS), pl.ds(col, 2 * HEAD)]
        qs = q_ref[pl.ds(q_at, QROWS), pl.ds(col, 2 * HEAD)]
        zero = jnp.zeros_like(qs)
        both = jnp.concatenate(
            [jnp.where(lane < HEAD, qs, zero), jnp.where(lane >= HEAD, qs, zero)], axis=0
        )
        scores = lax.dot_general(keys, both, (((1,), (1,)), ((), ())), preferred_element_type=F32)
        mask = mask_ref[:, pl.ds(q_at, QROWS)]
        scores = scores + jnp.concatenate([mask, mask], axis=1)
        expd = jnp.exp(scores - jnp.max(scores, axis=0, keepdims=True))
        total = jnp.sum(expd, axis=0, keepdims=True)
        values = vt_ref[pl.ds(col, 2 * HEAD), pl.ds(q_at, KROWS)]
        mixed = jnp.dot(values, expd.astype(BF16), preferred_element_type=F32) / total
        mixed = jnp.concatenate([mixed[:HEAD, :QROWS], mixed[HEAD:, QROWS:]], axis=0)
        mixed_ref[pl.ds(q_at, QROWS), pl.ds(col, 2 * HEAD)] = mixed.T.astype(BF16)
        return carry

    lax.fori_loop(0, (SHARD // QROWS) * (HEADS // 2), attend_tile, 0)

    copies[2].wait()
    output = jnp.dot(mixed_ref[...], wo_ref[...], preferred_element_type=F32)
    output = output + emb_ref[CTX : CTX + SHARD, :].astype(F32)
    out_ref[...] = output.astype(BF16)


def layer(me, lens, own, up, down, k1, b1, k2, b2, gain, we, wh, wo, interpret=False):
    vmem = pl.BlockSpec(memory_space=pltpu.VMEM)
    any_spec = pl.BlockSpec(memory_space=pl.ANY)
    return pl.pallas_call(
        layer_kernel,
        out_shape=jax.ShapeDtypeStruct((SHARD, D), BF16),
        in_specs=[pl.BlockSpec(memory_space=pltpu.SMEM)] + [vmem] * 9 + [any_spec] * 3,
        out_specs=vmem,
        scratch_shapes=[
            pltpu.VMEM(we.shape, BF16),
            pltpu.VMEM(wh.shape, BF16),
            pltpu.VMEM(wo.shape, BF16),
            pltpu.VMEM((3, WIN, 256), BF16),
            pltpu.VMEM((3, 256, 256), BF16),
            pltpu.VMEM((WIN, PAIRS * CH), BF16),
            pltpu.VMEM((WIN, CH), F32),
            pltpu.VMEM((WIN, D), BF16),
            pltpu.VMEM((WIN, D), BF16),
            pltpu.VMEM((SHARD, D), BF16),
            pltpu.VMEM((WIN, D), BF16),
            pltpu.VMEM((D, WIN), BF16),
            pltpu.VMEM((KROWS, SHARD), F32),
            pltpu.VMEM((SHARD, D), BF16),
            pltpu.SemaphoreType.DMA((3,)),
        ],
        compiler_params=pltpu.CompilerParams(vmem_limit_bytes=56 * 1024 * 1024),
        interpret=interpret,
        name="layer",
    )(me, lens, own, up, down, k1, b1, k2, b2, gain, we, wh, wo)


def on_device(log_mel, lengths, k1, b1, k2, b2, we, gain, wh, wo):
    devices = lax.axis_size(AXES)
    me = lax.axis_index(AXES).astype(jnp.int32).reshape(1)
    own = log_mel.T
    ahead = [(i, i + 1) for i in range(devices - 1)]
    back = [(i + 1, i) for i in range(devices - 1)]
    up = lax.ppermute(own[:, CAP - SHARD :], AXES, ahead)
    down = lax.ppermute(own[:, : MARGIN + SPAN], AXES, back)
    return layer(
        me, lengths.T, own, up, down, k1, b1.reshape(1, -1), k2, b2.reshape(1, -1),
        gain.reshape(1, -1), we, wh, wo,
    )


def solution(mesh):
    return jax.shard_map(
        on_device,
        mesh=mesh,
        in_specs=(P(AXES, None), P(), P(), P(), P(), P(), P(), P(), P(), P()),
        out_specs=P(AXES, None),
        check_vma=False,
    )
```

profile of v0, /device:TPU:1, one launch (start us, length us, event | category | flops | bytes accessed | tf_op | source)
XLA Modules:
  0.0 71.5 jit_solution(7253943327943859369)
XLA Ops:
  0.0 1.0 %slice.8 = bf16[320,512]{1,0:T(8,128)(2,1)S(1)} slice(bf16[320,896]{1,0:T(8,128)(2,1)} %bitcast.6), slice={[0:320], [384:896]} | slice | bytes 655360 | tf_op jit(solution)/shard_map/slice | solution.py:257
  1.0 4.5 %collective-permute-start = (bf16[320,512]{1,0:T(8,128)(2,1)S(1)}, bf16[320,512]{1,0:T(8,128)(2,1)S(1)}, u32[]{:S(2)}, u32[]{:S(2)}) collective-permute-start(bf16[320,512]{1,0:T(8,128)(2,1)S(1)} %slice.8), channel_id=1, source_target_pairs={{0,1},{1,2},{2,3},{3,4},{4,5},{5,6},{6,7},{7,8},{8,9},{9,10},{10,1... | collective-permute-start | bytes 983048 | tf_op jit(solution)/shard_map/ppermute | solution.py:257
  5.5 0.9 %slice.9 = bf16[320,256]{1,0:T(8,128)(2,1)S(1)} slice(bf16[320,896]{1,0:T(8,128)(2,1)} %bitcast.7), slice={[0:320], [0:256]} | slice | bytes 327680 | tf_op jit(solution)/shard_map/slice | solution.py:258
  6.5 1.9 %collective-permute-start.1 = (bf16[320,256]{1,0:T(8,128)(2,1)S(1)}, bf16[320,256]{1,0:T(8,128)(2,1)S(1)}, u32[]{:S(2)}, u32[]{:S(2)}) collective-permute-start(bf16[320,256]{1,0:T(8,128)(2,1)S(1)} %slice.9), channel_id=1, source_target_pairs={{1,0},{2,1},{3,2},{4,3},{5,4},{6,5},{7,6},{8,7},{9,8},{10,9},{11,1... | collective-permute-start | bytes 491528 | tf_op jit(solution)/shard_map/ppermute | solution.py:258
  8.4 4.7 %collective-permute-done.1.down_ref = bf16[320,256]{1,0:T(8,128)(2,1)S(1)} collective-permute-done((bf16[320,256]{1,0:T(8,128)(2,1)S(1)}, bf16[320,256]{1,0:T(8,128)(2,1)S(1)}, u32[]{:S(2)}, u32[]{:S(2)}) %collective-permute-start.1) | collective-permute-done | bytes 163872 | tf_op jit(solution)/shard_map/ppermute | solution.py:258
  13.1 0.0 copy-start.1
  13.1 0.0 collective-permute-done.up_ref
  13.1 0.0 copy-start
  13.1 0.6 copy-done.1
  13.8 0.1 copy-done
  13.9 57.6 %layer.1 = bf16[512,1024]{1,0:T(8,128)(2,1)} custom-call(s32[1]{0:T(128)} %bitcast.me_ref, s32[4,32]{1,0:T(4,128)} %bitcast.10, bf16[320,896]{1,0:T(8,128)(2,1)} %bitcast.8, bf16[320,512]{1,0:T(8,128)(2,1)} %copy-done, bf16[320,256]{1,0:T(8,128)(2,1)} %copy-done.1, bf16[9,128]{1,0:T(8,128)(2,1)} %k1_ref.1, f32[1,128]{1,0:T(1,128)} %bitcast.11, ...), custom_call_target="tpu_custom_call" | custom-call | tf_op jit(solution)/shard_map/layer/pallas_call | solution.py:223
Async XLA Ops:
  1.0 12.1 %collective-permute-start = (bf16[320,512]{1,0:T(8,128)(2,1)S(1)}, bf16[320,512]{1,0:T(8,128)(2,1)S(1)}, u32[]{:S(2)}, u32[]{:S(2)}) collective-permute-start(bf16[320,512]{1,0:T(8,128)(2,1)S(1)} %slice.8), channel_id=1, source_target_pairs={{0,1},{1,2},{2,3},{3,4},{4,5},{5,6},{6,7},{7,8},{8,9},{9,10},{10,1... | collective-permute-start | bytes 983048 | tf_op jit(solution)/shard_map/ppermute | solution.py:257
  6.5 6.6 %collective-permute-start.1 = (bf16[320,256]{1,0:T(8,128)(2,1)S(1)}, bf16[320,256]{1,0:T(8,128)(2,1)S(1)}, u32[]{:S(2)}, u32[]{:S(2)}) collective-permute-start(bf16[320,256]{1,0:T(8,128)(2,1)S(1)} %slice.9), channel_id=1, source_target_pairs={{1,0},{2,1},{3,2},{4,3},{5,4},{6,5},{7,6},{8,7},{9,8},{10,9},{11,1... | collective-permute-start | bytes 491528 | tf_op jit(solution)/shard_map/ppermute | solution.py:258
  13.1 0.7 copy-start.1
  13.1 0.8 %copy-start = (bf16[320,512]{1,0:T(8,128)(2,1)}, bf16[320,512]{1,0:T(8,128)(2,1)S(1)}, u32[]{:S(2)}) copy-start(bf16[320,512]{1,0:T(8,128)(2,1)S(1)} %collective-permute-done.up_ref) | copy-start | bytes 983044
where the time goes:
time: 72.7 us; the launch traced here: 71.5 us
  Pallas kernels  57.6 us (79%)
  starting transfers between devices  6.46 us (9%)
  waiting for transfers between devices  4.71 us (6%)
  local copies, waits for them, and re-layouts  2.7 us (4%)
    pallas_call x1, Pallas kernels, layer(): pl.pallas_call(layer_kernel, out_shape=jax.ShapeDtypeStruct((SHARD, D), B...  57.6 us
    ppermute x1, waiting for transfers between devices, on_device(): down = lax.ppermute(own[:, :MARGIN + SPAN], AXES, back)  4.7 us
    ppermute x1, starting transfers between devices, on_device(): up = lax.ppermute(own[:, CAP - SHARD:], AXES, ahead)  4.54 us
    ppermute x1, starting transfers between devices, on_device(): down = lax.ppermute(own[:, :MARGIN + SPAN], AXES, back)  1.92 us
  transfers between devices with their start and end apart: 2, of which 1 were waited for; matrix products, arithmetic and copies ran while one was open for 1% of the time, Pallas kernels for 0%

commit v1 on v0

--- a/solution.py
+++ b/solution.py
@@ -80,38 +80,45 @@
 def second_weights(k2_ref, w2_ref):
     for tap in range(3):
         base = tap * 3 * CH
-        w2_ref[tap, :, :CH] = k2_ref[base + CH : base + 3 * CH, :]
-        w2_ref[tap, :CH, CH:] = jnp.zeros((CH, CH), BF16)
-        w2_ref[tap, CH:, CH:] = k2_ref[base : base + CH, :]
-
-
-def first_weights(pair, k1, bias_rows):
-    row = iota((3 * MEL, CH), 0)
-    frame_row = [(row >= MEL * a) & (row < MEL * (a + 1)) for a in range(3)]
-    bin_row = row - jnp.where(row >= 2 * MEL, 2 * MEL, jnp.where(row >= MEL, MEL, 0))
-    taps = []
-    for b in range(3):
-        taps.append(
-            jnp.where(
-                frame_row[0],
-                k1[b : b + 1],
-                jnp.where(frame_row[1], k1[3 + b : 4 + b], k1[6 + b : 7 + b]),
-            )
-        )
-    halves = []
-    for half in range(2):
-        at = bin_row - (2 * (2 * pair + half) - 1)
-        value = jnp.where(at == 0, taps[0], jnp.where(at == 1, taps[1], 0.0))
-        value = jnp.where(at == 2, taps[2], value)
-        halves.append(jnp.concatenate([value, bias_rows], axis=0))
-    return jnp.concatenate(halves, axis=1).astype(BF16)
+        row = tap * 2 * CH
+        w2_ref[row : row + 2 * CH, :CH] = k2_ref[base + CH : base + 3 * CH, :]
+        w2_ref[row : row + CH, CH:] = jnp.zeros((CH, CH), BF16)
+        w2_ref[row + CH : row + 2 * CH, CH:] = k2_ref[base : base + CH, :]
+
+
+def first_tiles(k1, odd):
+    row = iota((8, CH), 0)
+    tiles = []
+    for at in (0,) if odd else (-1, 0):
+        tile = []
+        for tap in range(3):
+            halves = []
+            for half in range(2):
+                low = (4 if odd else 0) + 2 * half - 1 - 8 * at
+                value = jnp.zeros((8, CH), F32)
+                for b in range(3):
+                    value = jnp.where(row == low + b, k1[3 * tap + b : 3 * tap + b + 1], value)
+                halves.append(value)
+            tile.append(jnp.concatenate(halves, axis=1))
+        tiles.append((at, tile))
+    return tiles
+
+
+def place_tiles(w1_ref, slot, step, tiles):
+    first = 8 * (step + 1)
+    for at, tile in tiles:
+        for tap in range(3):
+            w1_ref[slot, tap, pl.ds(pl.multiple_of(first + 8 * at, 8), 8), :] = tile[tap]
+    clear = first + 8 * (tiles[0][0] - 1)
+    for tap in range(3):
+        w1_ref[slot, tap, pl.ds(pl.multiple_of(jnp.maximum(clear, 0), 8), 8), :] = jnp.zeros((8, 2 * CH), F32)
 
 
 def layer_kernel(
     me_ref, len_ref, own_ref, up_ref, down_ref, k1_ref, b1_ref, k2_ref, b2_ref, gain_ref,
     we_hbm, wh_hbm, wo_hbm, out_ref,
-    we_ref, wh_ref, wo_ref, x_ref, w2_ref, sec_ref, low_ref, emb_ref, norm_ref,
-    q_ref, k_ref, vt_ref, mask_ref, mixed_ref, sems,
+    we_ref, wh_ref, wo_ref, x_ref, w1_ref, w2_ref, h_ref, sec_ref, low_ref, emb_ref, norm_ref,
+    q_ref, k_ref, vt_ref, mask_ref, score_ref, peak_ref, prob_ref, mixed_ref, sems,
 ):
     copies = [
         pltpu.make_async_copy(src, dst, sems.at[i])
@@ -130,25 +137,51 @@
     row = iota((16, CH), 0)
     bias_rows = jnp.where(row == 0, b_high, jnp.where(row == 1, b_mid, b_low))
     bias_rows = jnp.where(row < 3, bias_rows, jnp.where(row == 3, -1e30, 0.0))
+    bias_rows = jnp.concatenate([bias_rows, bias_rows], axis=1)
     k1 = k1_ref[...].astype(F32)
     bias_2 = b2_ref[...]
-
-    def conv_pair(pair, carry):
-        w1 = first_weights(pair, k1, bias_rows)
-        for t in range(WIN // ROWS):
-            rows = slice(t * ROWS, (t + 1) * ROWS)
-            acc = None
-            for tap in range(3):
-                h = jnp.dot(x_ref[tap, rows, :], w1, preferred_element_type=F32)
-                h = jnp.maximum(h, 0.0).astype(BF16)
-                part = jnp.dot(h, w2_ref[tap], preferred_element_type=F32)
-                acc = part if acc is None else acc + part
-            value = jnp.maximum(acc[:, :CH] + low_ref[rows, :] + bias_2, 0.0).astype(BF16)
-            low_ref[rows, :] = acc[:, CH:]
-            sec_ref[rows, pl.ds(pl.multiple_of(pair * CH, CH), CH)] = value
+    tiles = [first_tiles(k1, odd) for odd in range(2)]
+    w1_ref[...] = jnp.zeros_like(w1_ref)
+    chunks = [slice(t * ROWS, (t + 1) * ROWS) for t in range(WIN // ROWS)]
+
+    def conv_first(slot, step, rows, w1):
+        for tap in range(3):
+            h = jnp.dot(x_ref[tap, rows, :], w1, preferred_element_type=F32)
+            h_ref[slot, rows, tap * 2 * CH : (tap + 1) * 2 * CH] = jnp.maximum(h, 0.0).astype(BF16)
+
+    def conv_second(slot, pair, rows):
+        acc = jnp.dot(h_ref[slot, rows, :], w2_ref[...], preferred_element_type=F32)
+        value = jnp.maximum(acc[:, :CH] + low_ref[rows, :] + bias_2, 0.0).astype(BF16)
+        low_ref[rows, :] = acc[:, CH:]
+        sec_ref[rows, pl.ds(pl.multiple_of(pair * CH, CH), CH)] = value
+
+    def first_matrix(slot, step):
+        place_tiles(w1_ref, slot, step, tiles[slot])
+        taps = w1_ref[slot, :, 8 : 8 + MEL, :].reshape(3 * MEL, 2 * CH)
+        return jnp.concatenate([taps, bias_rows], axis=0).astype(BF16)
+
+    def conv_pairs(step, last):
+        w1 = first_matrix(1, step)
+        for rows in chunks:
+            conv_first(1, step, rows, w1)
+            conv_second(0, 2 * step, rows)
+        if not last:
+            w1 = first_matrix(0, step + 1)
+        for rows in chunks:
+            if not last:
+                conv_first(0, step + 1, rows, w1)
+            conv_second(1, 2 * step + 1, rows)
+
+    w1 = first_matrix(0, 0)
+    for rows in chunks:
+        conv_first(0, 0, rows, w1)
+
+    def conv_step(step, carry):
+        conv_pairs(step, False)
         return carry
 
-    lax.fori_loop(0, PAIRS, conv_pair, 0)
+    lax.fori_loop(0, PAIRS // 2 - 1, conv_step, 0)
+    conv_pairs(PAIRS // 2 - 1, True)
 
     copies[0].wait()
     gain = gain_ref[...]
@@ -186,30 +219,63 @@
         mask_ref[:, cols] = jnp.where(seen, 0.0, -jnp.inf)
 
     lane = iota((QROWS, 2 * HEAD), 1)
-
-    def attend_tile(step, carry):
-        i = step // (HEADS // 2)
-        pair = step % (HEADS // 2)
-        q_at = pl.multiple_of(i * QROWS, QROWS)
-        col = pl.multiple_of(pair * 2 * HEAD, 2 * HEAD)
-        keys = k_ref[pl.ds(q_at, KROWS), pl.ds(col, 2 * HEAD)]
+    pairs = HEADS // 2
+    steps = (SHARD // QROWS) * pairs
+    summing = jnp.ones((16, KROWS), BF16)
+
+    def places(step):
+        q_at = pl.multiple_of((step // pairs) * QROWS, QROWS)
+        col = pl.multiple_of((step % pairs) * 2 * HEAD, 2 * HEAD)
+        return q_at, col
+
+    def score(slot, step):
+        q_at, col = places(step)
         qs = q_ref[pl.ds(q_at, QROWS), pl.ds(col, 2 * HEAD)]
         zero = jnp.zeros_like(qs)
         both = jnp.concatenate(
             [jnp.where(lane < HEAD, qs, zero), jnp.where(lane >= HEAD, qs, zero)], axis=0
         )
+        keys = k_ref[pl.ds(q_at, KROWS), pl.ds(col, 2 * HEAD)]
         scores = lax.dot_general(keys, both, (((1,), (1,)), ((), ())), preferred_element_type=F32)
         mask = mask_ref[:, pl.ds(q_at, QROWS)]
         scores = scores + jnp.concatenate([mask, mask], axis=1)
-        expd = jnp.exp(scores - jnp.max(scores, axis=0, keepdims=True))
-        total = jnp.sum(expd, axis=0, keepdims=True)
+        score_ref[slot] = scores
+        peak_ref[slot] = jnp.max(scores, axis=0, keepdims=True)
+
+    def weigh(slot):
+        prob_ref[slot] = jnp.exp(score_ref[slot] - peak_ref[slot]).astype(BF16)
+
+    def mix(slot, step):
+        q_at, col = places(step)
         values = vt_ref[pl.ds(col, 2 * HEAD), pl.ds(q_at, KROWS)]
-        mixed = jnp.dot(values, expd.astype(BF16), preferred_element_type=F32) / total
+        values = jnp.concatenate([values, summing], axis=0)
+        mixed = jnp.dot(values, prob_ref[slot], preferred_element_type=F32)
+        mixed = mixed[: 2 * HEAD] / mixed[2 * HEAD : 2 * HEAD + 1]
         mixed = jnp.concatenate([mixed[:HEAD, :QROWS], mixed[HEAD:, QROWS:]], axis=0)
         mixed_ref[pl.ds(q_at, QROWS), pl.ds(col, 2 * HEAD)] = mixed.T.astype(BF16)
+
+    def attend_two(it, carry):
+        for slot in range(2):
+            mix(slot, 2 * it + slot)
+        for slot in range(2):
+            weigh(slot)
+        for slot in range(2):
+            score(slot, 2 * it + 4 + slot)
         return carry
 
-    lax.fori_loop(0, (SHARD // QROWS) * (HEADS // 2), attend_tile, 0)
+    for slot in range(2):
+        score(slot, slot)
+    for slot in range(2):
+        weigh(slot)
+    for slot in range(2):
+        score(slot, 2 + slot)
+    lax.fori_loop(0, steps // 2 - 2, attend_two, 0)
+    for slot in range(2):
+        mix(slot, steps - 4 + slot)
+    for slot in range(2):
+        weigh(slot)
+    for slot in range(2):
+        mix(slot, steps - 2 + slot)
 
     copies[2].wait()
     output = jnp.dot(mixed_ref[...], wo_ref[...], preferred_element_type=F32)
@@ -230,7 +296,9 @@
             pltpu.VMEM(wh.shape, BF16),
             pltpu.VMEM(wo.shape, BF16),
             pltpu.VMEM((3, WIN, 256), BF16),
-            pltpu.VMEM((3, 256, 256), BF16),
+            pltpu.VMEM((2, 3, MEL + 16, 2 * CH), F32),
+            pltpu.VMEM((3 * 2 * CH, 2 * CH), BF16),
+            pltpu.VMEM((2, WIN, 3 * 2 * CH), BF16),
             pltpu.VMEM((WIN, PAIRS * CH), BF16),
             pltpu.VMEM((WIN, CH), F32),
             pltpu.VMEM((WIN, D), BF16),
@@ -239,6 +307,9 @@
             pltpu.VMEM((WIN, D), BF16),
             pltpu.VMEM((D, WIN), BF16),
             pltpu.VMEM((KROWS, SHARD), F32),
+            pltpu.VMEM((2, KROWS, 2 * QROWS), F32),
+            pltpu.VMEM((2, 1, 2 * QROWS), F32),
+            pltpu.VMEM((2, KROWS, 2 * QROWS), BF16),
             pltpu.VMEM((SHARD, D), BF16),
             pltpu.SemaphoreType.DMA((3,)),
         ],

time: 72.7 us -> 53.5 us (0.74)
  the two profiles are of different devices: /device:TPU:1 before, /device:TPU:23 now
where the time goes in v1:
time: 53.5 us; the launch traced here: 53.3 us
  Pallas kernels  38.4 us (72%)
  waiting for transfers between devices  6.5 us (12%)
  starting transfers between devices  5.6 us (10%)
  local copies, waits for them, and re-layouts  2.7 us (5%)
    pallas_call x1, Pallas kernels, layer(): pl.pallas_call(layer_kernel, out_shape=jax.ShapeDtypeStruct((SHARD, D), B...  38.4 us
    ppermute x1, waiting for transfers between devices, on_device(): down = lax.ppermute(own[:, :MARGIN + SPAN], AXES, back)  6.5 us
    ppermute x1, starting transfers between devices, on_device(): up = lax.ppermute(own[:, CAP - SHARD:], AXES, ahead)  3.68 us
    ppermute x1, starting transfers between devices, on_device(): down = lax.ppermute(own[:, :MARGIN + SPAN], AXES, back)  1.92 us
  transfers between devices with their start and end apart: 2, of which 1 were waited for; matrix products, arithmetic and copies ran while one was open for 2% of the time, Pallas kernels for 0%

profile of v1, /device:TPU:23, one launch (start us, length us, event | category | flops | bytes accessed | tf_op | source)
XLA Modules:
  0.0 53.3 jit_solution(2713348689212109675)
XLA Ops:
  0.0 1.0 %slice.8 = bf16[320,512]{1,0:T(8,128)(2,1)S(1)} slice(bf16[320,896]{1,0:T(8,128)(2,1)} %bitcast.6), slice={[0:320], [384:896]} | slice | bytes 655360 | tf_op jit(solution)/shard_map/slice | solution.py:328
  1.0 3.7 %collective-permute-start = (bf16[320,512]{1,0:T(8,128)(2,1)S(1)}, bf16[320,512]{1,0:T(8,128)(2,1)S(1)}, u32[]{:S(2)}, u32[]{:S(2)}) collective-permute-start(bf16[320,512]{1,0:T(8,128)(2,1)S(1)} %slice.8), channel_id=1, source_target_pairs={{0,1},{1,2},{2,3},{3,4},{4,5},{5,6},{6,7},{7,8},{8,9},{9,10},{10,1... | collective-permute-start | bytes 983048 | tf_op jit(solution)/shard_map/ppermute | solution.py:328
  4.7 0.9 %slice.9 = bf16[320,256]{1,0:T(8,128)(2,1)S(1)} slice(bf16[320,896]{1,0:T(8,128)(2,1)} %bitcast.7), slice={[0:320], [0:256]} | slice | bytes 327680 | tf_op jit(solution)/shard_map/slice | solution.py:329
  5.6 1.9 %collective-permute-start.1 = (bf16[320,256]{1,0:T(8,128)(2,1)S(1)}, bf16[320,256]{1,0:T(8,128)(2,1)S(1)}, u32[]{:S(2)}, u32[]{:S(2)}) collective-permute-start(bf16[320,256]{1,0:T(8,128)(2,1)S(1)} %slice.9), channel_id=1, source_target_pairs={{1,0},{2,1},{3,2},{4,3},{5,4},{6,5},{7,6},{8,7},{9,8},{10,9},{11,1... | collective-permute-start | bytes 491528 | tf_op jit(solution)/shard_map/ppermute | solution.py:329
  7.6 6.5 %collective-permute-done.1.down_ref = bf16[320,256]{1,0:T(8,128)(2,1)S(1)} collective-permute-done((bf16[320,256]{1,0:T(8,128)(2,1)S(1)}, bf16[320,256]{1,0:T(8,128)(2,1)S(1)}, u32[]{:S(2)}, u32[]{:S(2)}) %collective-permute-start.1) | collective-permute-done | bytes 163872 | tf_op jit(solution)/shard_map/ppermute | solution.py:329
  14.1 0.0 copy-start.1
  14.1 0.0 collective-permute-done.up_ref
  14.1 0.0 copy-start
  14.1 0.6 %copy-done.1 = bf16[320,256]{1,0:T(8,128)(2,1)} copy-done((bf16[320,256]{1,0:T(8,128)(2,1)}, bf16[320,256]{1,0:T(8,128)(2,1)S(1)}, u32[]{:S(2)}) %copy-start.1) | copy-done | bytes 163864
  14.7 0.1 copy-done
  14.8 38.4 %layer.1 = bf16[512,1024]{1,0:T(8,128)(2,1)} custom-call(s32[1]{0:T(128)} %bitcast.me_ref, s32[4,32]{1,0:T(4,128)} %bitcast.10, bf16[320,896]{1,0:T(8,128)(2,1)} %bitcast.8, bf16[320,512]{1,0:T(8,128)(2,1)} %copy-done, bf16[320,256]{1,0:T(8,128)(2,1)} %copy-done.1, bf16[9,128]{1,0:T(8,128)(2,1)} %k1_ref.1, f32[1,128]{1,0:T(1,128)} %bitcast.11, ...), custom_call_target="tpu_custom_call" | custom-call | tf_op jit(solution)/shard_map/layer/pallas_call | solution.py:289
Async XLA Ops:
  1.0 13.1 %collective-permute-start = (bf16[320,512]{1,0:T(8,128)(2,1)S(1)}, bf16[320,512]{1,0:T(8,128)(2,1)S(1)}, u32[]{:S(2)}, u32[]{:S(2)}) collective-permute-start(bf16[320,512]{1,0:T(8,128)(2,1)S(1)} %slice.8), channel_id=1, source_target_pairs={{0,1},{1,2},{2,3},{3,4},{4,5},{5,6},{6,7},{7,8},{8,9},{9,10},{10,1... | collective-permute-start | bytes 983048 | tf_op jit(solution)/shard_map/ppermute | solution.py:328
  5.6 8.4 %collective-permute-start.1 = (bf16[320,256]{1,0:T(8,128)(2,1)S(1)}, bf16[320,256]{1,0:T(8,128)(2,1)S(1)}, u32[]{:S(2)}, u32[]{:S(2)}) collective-permute-start(bf16[320,256]{1,0:T(8,128)(2,1)S(1)} %slice.9), channel_id=1, source_target_pairs={{1,0},{2,1},{3,2},{4,3},{5,4},{6,5},{7,6},{8,7},{9,8},{10,9},{11,1... | collective-permute-start | bytes 491528 | tf_op jit(solution)/shard_map/ppermute | solution.py:329
  14.1 0.7 %copy-start.1 = (bf16[320,256]{1,0:T(8,128)(2,1)}, bf16[320,256]{1,0:T(8,128)(2,1)S(1)}, u32[]{:S(2)}) copy-start(bf16[320,256]{1,0:T(8,128)(2,1)S(1)} %collective-permute-done.1.down_ref) | copy-start | bytes 491524
  14.1 0.8 %copy-start = (bf16[320,512]{1,0:T(8,128)(2,1)}, bf16[320,512]{1,0:T(8,128)(2,1)S(1)}, u32[]{:S(2)}) copy-start(bf16[320,512]{1,0:T(8,128)(2,1)S(1)} %collective-permute-done.up_ref) | copy-start | bytes 983044

commit v2 on v1

v2 whole, which is shorter than its diff:
```python
import jax
import jax.numpy as jnp
from jax import lax
from jax.experimental import pallas as pl
from jax.experimental.pallas import tpu as pltpu
from jax.sharding import PartitionSpec as P

HEADS = 16
SPAN = 64
LEFT_SPANS = 4
CTX = 320
SHARD = 512
MARGIN = 192
CAP = 896
WIN = CTX + SHARD + SPAN
MEL = 80
CH = 128
PAIRS = MEL // 4
D = 1024
HEAD = D // HEADS
ROWS = 448
LEAD = 16
EARLY = 384
LATE = 256
QROWS = 128
KROWS = 512
AXES = ("seq", "inner")
F32 = jnp.float32
BF16 = jnp.bfloat16


def iota(shape, dim):
    return lax.broadcasted_iota(jnp.int32, shape, dim)


def frame_facts(me, len_ref, low, count):
    lens = len_ref[...].astype(F32)
    utts, devices = lens.shape
    lane = iota((devices, devices), 1)
    sub = iota((devices, devices), 0)
    owner_len = jnp.sum(lens, axis=0, keepdims=True)
    lane_row = iota((1, devices), 1)
    own_low = jnp.sum(jnp.where(lane_row < me, owner_len, 0.0), axis=1, keepdims=True)
    own_high = own_low + jnp.sum(jnp.where(lane_row == me, owner_len, 0.0), axis=1, keepdims=True)
    start = jnp.sum(jnp.where(lane < sub, owner_len, 0.0), axis=1, keepdims=True)
    total = (devices * SHARD) * 1.0
    frame = (iota((1, count), 1) + (me * SHARD - CTX + low)).astype(F32)
    begin = jnp.zeros((1, count), F32)
    end = jnp.full((1, count), total, F32)
    for u in range(utts):
        reached = start <= frame
        begin = jnp.maximum(begin, jnp.max(jnp.where(reached, start, 0.0), axis=0, keepdims=True))
        end = jnp.minimum(end, jnp.min(jnp.where(reached, total, start), axis=0, keepdims=True))
        start = start + jnp.sum(
            jnp.where(lane == sub, lens[u : u + 1, :], 0.0), axis=1, keepdims=True
        )
    return frame, begin, end, own_low, own_high


def frame_taps(raw, fresh, x_ref, joined_ref):
    count = raw.shape[1]
    ones = jnp.where(iota((16, count), 0) < 3, 1.0, 0.0)
    head = jnp.where(fresh, 0.0, pltpu.roll(raw[3 * MEL :], 1, 1))
    x_ref[0] = jnp.concatenate([head, raw[: 2 * MEL], ones], axis=0).T.astype(BF16)
    x_ref[1] = jnp.concatenate([raw[MEL:], ones], axis=0).T.astype(BF16)
    joined_ref[...] = jnp.broadcast_to(jnp.where(fresh, 0.0, 1.0), (CH, count)).T


def second_weights(k2_ref, w2_ref):
    for tap in range(3):
        base = tap * 3 * CH
        row = tap * 2 * CH
        w2_ref[row : row + 2 * CH, :CH] = k2_ref[base + CH : base + 3 * CH, :]
        w2_ref[row : row + CH, CH:] = jnp.zeros((CH, CH), BF16)
        w2_ref[row + CH : row + 2 * CH, CH:] = k2_ref[base : base + CH, :]


def first_tiles(k1, odd):
    row = iota((8, CH), 0)
    tiles = []
    for at in (0,) if odd else (-1, 0):
        tile = []
        for tap in range(3):
            halves = []
            for half in range(2):
                low = (4 if odd else 0) + 2 * half - 1 - 8 * at
                value = jnp.zeros((8, CH), F32)
                for b in range(3):
                    value = jnp.where(row == low + b, k1[3 * tap + b : 3 * tap + b + 1], value)
                halves.append(value)
            tile.append(jnp.concatenate(halves, axis=1))
        tiles.append((at, tile))
    return tiles


def place_tiles(w1_ref, slot, step, tiles):
    first = 8 * (step + 1)
    for at, tile in tiles:
        for tap in range(3):
            w1_ref[slot, tap, first + 8 * at : first + 8 * at + 8, :] = tile[tap]
    clear = first + 8 * (tiles[0][0] - 1)
    if clear >= 0:
        for tap in range(3):
            w1_ref[slot, tap, clear : clear + 8, :] = jnp.zeros((8, 2 * CH), F32)


def convolve(
    chunks, k1_ref, b1_ref, k2_ref, b2_ref, x_ref, joined_ref, w1_ref, w2_ref, h_ref, low_ref, sec_ref, done=None
):
    second_weights(k2_ref, w2_ref)
    low_ref[...] = jnp.zeros_like(low_ref)
    bias = b1_ref[...]
    b_high = bias.astype(BF16).astype(F32)
    b_mid = (bias - b_high).astype(BF16).astype(F32)
    b_low = bias - b_high - b_mid
    row = iota((16, CH), 0)
    bias_rows = jnp.where(row == 0, b_high, jnp.where(row == 1, b_mid, b_low))
    bias_rows = jnp.where(row < 3, bias_rows, 0.0)
    bias_rows = jnp.concatenate([bias_rows, bias_rows], axis=1)
    k1 = k1_ref[...].astype(F32)
    bias_2 = b2_ref[...]
    tiles = [first_tiles(k1, odd) for odd in range(2)]
    w1_ref[...] = jnp.zeros_like(w1_ref)

    def conv_first(slot, chunk, w1):
        at, lead, count, _ = chunk
        rows = slice(at, at + count)
        even = jnp.dot(x_ref[0, rows, :], w1, preferred_element_type=F32)
        h_ref[slot, rows, 2 * CH : 4 * CH] = jnp.maximum(even, 0.0).astype(BF16)
        odd = jnp.dot(x_ref[1, at - lead : at + count, :], w1, preferred_element_type=F32)
        odd = jnp.maximum(odd, 0.0)
        h_ref[slot, rows, 4 * CH :] = odd[lead:].astype(BF16)
        before = pltpu.roll(odd, 1, 0)[lead:]
        joined = joined_ref[rows, :]
        before = before * jnp.concatenate([joined, joined], axis=1)
        h_ref[slot, rows, : 2 * CH] = before.astype(BF16)

    def conv_second(slot, chunk, pair):
        at, _, count, to = chunk
        rows = slice(at, at + count)
        acc = jnp.dot(h_ref[slot, rows, :], w2_ref[...], preferred_element_type=F32)
        value = jnp.maximum(acc[:, :CH] + low_ref[rows, :] + bias_2, 0.0).astype(BF16)
        low_ref[rows, :] = acc[:, CH:]
        sec_ref[pl.ds(to, count), pair * CH : (pair + 1) * CH] = value

    def first_matrix(slot, step):
        place_tiles(w1_ref, slot, step, tiles[slot])
        taps = w1_ref[slot, :, 8 : 8 + MEL, :].reshape(3 * MEL, 2 * CH)
        return jnp.concatenate([taps, bias_rows], axis=0).astype(BF16)

    def conv_pairs(step, last):
        w1 = first_matrix(1, step)
        for chunk in chunks:
            conv_first(1, chunk, w1)
            conv_second(0, chunk, 2 * step)
        if not last:
            w1 = first_matrix(0, step + 1)
        for chunk in chunks:
            if not last:
                conv_first(0, chunk, w1)
            conv_second(1, chunk, 2 * step + 1)

    w1 = first_matrix(0, 0)
    for chunk in chunks:
        conv_first(0, chunk, w1)

    for step in range(PAIRS // 2):
        conv_pairs(step, step == PAIRS // 2 - 1)
        if done is not None:
            done(step)


def fetch(sources, targets, sems):
    copies = [
        pltpu.make_async_copy(src, dst, sems.at[i])
        for i, (src, dst) in enumerate(zip(sources, targets, strict=True))
    ]
    for copy in copies:
        copy.start()
    return copies


def early_rows(me):
    return jnp.where(lax.rem(me, 2) == 1, 256, 512)


def early_kernel(
    me_ref, chip_ref, len_hbm, own_hbm, k1_hbm, b1_hbm, k2_hbm, b2_hbm, out_hbm,
    len_ref, own_ref, k1_ref, b1_ref, k2_ref, b2_ref, sems,
    x_ref, joined_ref, w1_ref, w2_ref, h_ref, low_ref, sec_ref, out_sems,
):
    me = me_ref[0]
    first = early_rows(me) - 128
    copies = fetch(
        (len_hbm, own_hbm.at[:, pl.ds(pl.multiple_of(first - 128, 128), EARLY + 128)])
        + (k1_hbm, b1_hbm, k2_hbm, b2_hbm),
        (len_ref, own_ref, k1_ref, b1_ref, k2_ref, b2_ref),
        sems,
    )
    copies[0].wait()
    frame, begin, _, own_low, own_high = frame_facts(me, len_ref, first, EARLY + 128)
    chip = chip_ref[...].astype(F32)
    edge = jnp.where(lax.rem(me, 2) == 1, chip[:, 384:], chip[:, :128])
    other = jnp.concatenate([chip[:, 128:384], edge, chip[:, 128:256]], axis=1)
    owned = (frame >= own_low) & (frame < own_high)
    for copy in copies[1:]:
        copy.wait()
    raw = jnp.where(owned, own_ref[...].astype(F32), other)
    frame_taps(raw, begin == frame, x_ref, joined_ref)
    sent = []

    def send(step):
        cols = slice(step * 2 * CH, (step + 1) * 2 * CH)
        sent.append(pltpu.make_async_copy(sec_ref.at[:, cols], out_hbm.at[:, cols], out_sems.at[step]))
        sent[-1].start()

    convolve(
        [(128, LEAD, EARLY, 0)], k1_ref, b1_ref, k2_ref, b2_ref,
        x_ref, joined_ref, w1_ref, w2_ref, h_ref, low_ref, sec_ref, send,
    )
    for copy in sent:
        copy.wait()


def layer_kernel(
    me_ref, cross_ref, chip_ref, early_hbm, len_hbm, own_hbm, k1_hbm, b1_hbm, k2_hbm, b2_hbm, gain_hbm,
    we_hbm, wh_hbm, wo_hbm, out_hbm,
    len_ref, own_ref, k1_ref, b1_ref, k2_ref, b2_ref, gain_ref,
    we_ref, wh_ref, wo_ref, sems,
    x_ref, joined_ref, w1_ref, w2_ref, h_ref, low_ref, sec_ref, emb_ref, norm_ref,
    q_ref, k_ref, vt_ref, mask_ref, score_ref, peak_ref, prob_ref, mixed_ref, out_ref, out_sems,
):
    me = me_ref[0]
    odd = lax.rem(me, 2) == 1
    late = pl.multiple_of(jnp.where(odd, 640, 256), 128)
    late_own = pl.multiple_of(late - 256, 128)
    early = pl.multiple_of(early_rows(me), 128)
    copies = fetch(
        (len_hbm, own_hbm.at[:, :128], own_hbm.at[:, pl.ds(late_own, LATE + 128)])
        + (k1_hbm, b1_hbm, k2_hbm, b2_hbm, gain_hbm, we_hbm, early_hbm, wh_hbm, wo_hbm),
        (len_ref, own_ref.at[:, :128], own_ref.at[:, 128:])
        + (k1_ref, b1_ref, k2_ref, b2_ref, gain_ref, we_ref, sec_ref.at[pl.ds(early, EARLY), :], wh_ref, wo_ref),
        sems,
    )
    for copy in copies[:8]:
        copy.wait()
    copies = copies[8:]
    frame, begin, _, own_low, _ = frame_facts(me, len_ref, 0, 256)
    cross = cross_ref[...].astype(F32)
    up = jnp.where(odd, chip_ref[:, :256].astype(F32), cross[:, :256])
    raw = jnp.concatenate(
        [up[:, :128], jnp.where(frame[:, 128:] >= own_low, own_ref[:, :128].astype(F32), up[:, 128:])],
        axis=1,
    )
    late_frame, late_begin, _, own_low, own_high = frame_facts(me, len_ref, late - 128, LATE + 128)
    other = jnp.where(odd, jnp.concatenate([cross[:, :128], cross[:, :256]], axis=1), cross[:, 128:])
    owned = (late_frame >= own_low) & (late_frame < own_high)
    raw = jnp.concatenate([raw, jnp.where(owned, own_ref[:, 128:].astype(F32), other)], axis=1)
    fresh = jnp.concatenate([begin, late_begin], axis=1) == jnp.concatenate([frame, late_frame], axis=1)
    frame_taps(raw, fresh, x_ref, joined_ref)
    convolve(
        [(0, 0, 256, 0), (384, LEAD, LATE, late)], k1_ref, b1_ref, k2_ref, b2_ref,
        x_ref, joined_ref, w1_ref, w2_ref, h_ref, low_ref, sec_ref,
    )

    copies[0].wait()
    copies[1].wait()
    gain = gain_ref[...]
    for t in range(WIN // ROWS):
        rows = slice(t * ROWS, (t + 1) * ROWS)
        emb = jnp.dot(sec_ref[rows, :], we_ref[...], preferred_element_type=F32).astype(BF16)
        emb_ref[rows, :] = emb
        values = emb.astype(F32)
        center = values - jnp.mean(values, axis=1, keepdims=True)
        spread = jnp.mean(center * center, axis=1, keepdims=True)
        norm_ref[rows, :] = (center * lax.rsqrt(spread + 1e-05) * gain).astype(BF16)

    copies[2].wait()
    q = jnp.dot(norm_ref[CTX : CTX + SHARD, :], wh_ref[:, :D], preferred_element_type=F32)
    q_ref[...] = q.astype(BF16) * (HEAD**-0.5)
    for t in range(WIN // ROWS):
        rows = slice(t * ROWS, (t + 1) * ROWS)
        k = jnp.dot(norm_ref[rows, :], wh_ref[:, D : 2 * D], preferred_element_type=F32)
        k_ref[rows, :] = k.astype(BF16)
    for t in range(WIN // 128):
        rows = slice(t * 128, (t + 1) * 128)
        v = jnp.dot(norm_ref[rows, :], wh_ref[:, 2 * D :], preferred_element_type=F32)
        vt_ref[:, rows] = v.T.astype(BF16)

    query, q_begin, q_end, _, _ = frame_facts(me, len_ref, CTX, SHARD)
    span_at = jnp.floor((query - q_begin) * (1.0 / SPAN)) * SPAN
    key_low = q_begin + jnp.maximum(span_at - LEFT_SPANS * SPAN, 0.0)
    key_high = jnp.minimum(q_begin + span_at + SPAN, q_end)
    first_frame = (me_ref[0] * SHARD - CTX).astype(F32)
    for i in range(SHARD // QROWS):
        cols = slice(i * QROWS, (i + 1) * QROWS)
        key = iota((KROWS, QROWS), 0).astype(F32) + (first_frame + i * QROWS)
        seen = (key >= key_low[:, cols]) & (key < key_high[:, cols])
        mask_ref[:, cols] = jnp.where(seen, 0.0, -jnp.inf)

    lane = iota((QROWS, 2 * HEAD), 1)
    pairs = HEADS // 2
    steps = (SHARD // QROWS) * pairs
    summing = jnp.ones((16, KROWS), BF16)

    def places(step):
        q_at = (step // pairs) * QROWS
        col = (step % pairs) * 2 * HEAD
        return q_at, col

    def score(slot, step):
        q_at, col = places(step)
        qs = q_ref[pl.ds(q_at, QROWS), pl.ds(col, 2 * HEAD)]
        zero = jnp.zeros_like(qs)
        both = jnp.concatenate(
            [jnp.where(lane < HEAD, qs, zero), jnp.where(lane >= HEAD, qs, zero)], axis=0
        )
        keys = k_ref[pl.ds(q_at, KROWS), pl.ds(col, 2 * HEAD)]
        scores = lax.dot_general(keys, both, (((1,), (1,)), ((), ())), preferred_element_type=F32)
        mask = mask_ref[:, pl.ds(q_at, QROWS)]
        scores = scores + jnp.concatenate([mask, mask], axis=1)
        score_ref[slot] = scores
        peak_ref[slot] = jnp.max(scores, axis=0, keepdims=True)

    def weigh(slot):
        prob_ref[slot] = jnp.exp(score_ref[slot] - peak_ref[slot]).astype(BF16)

    def mix(slot, step):
        q_at, col = places(step)
        values = vt_ref[pl.ds(col, 2 * HEAD), pl.ds(q_at, KROWS)]
        values = jnp.concatenate([values, summing], axis=0)
        mixed = jnp.dot(values, prob_ref[slot], preferred_element_type=F32)
        mixed = mixed[: 2 * HEAD] / mixed[2 * HEAD : 2 * HEAD + 1]
        mixed = jnp.concatenate([mixed[:HEAD, :QROWS], mixed[HEAD:, QROWS:]], axis=0)
        mixed_ref[pl.ds(q_at, QROWS), pl.ds(col, 2 * HEAD)] = mixed.T.astype(BF16)

    def attend_two(it):
        for slot in range(2):
            mix(slot, 2 * it + slot)
        for slot in range(2):
            weigh(slot)
        for slot in range(2):
            score(slot, 2 * it + 4 + slot)

    for slot in range(2):
        score(slot, slot)
    for slot in range(2):
        weigh(slot)
    for slot in range(2):
        score(slot, 2 + slot)
    for it in range(steps // 2 - 2):
        attend_two(it)
    for slot in range(2):
        mix(slot, steps - 4 + slot)
    for slot in range(2):
        weigh(slot)
    for slot in range(2):
        mix(slot, steps - 2 + slot)

    copies[3].wait()
    sent = []
    for t in range(2):
        rows = slice(t * SHARD // 2, (t + 1) * SHARD // 2)
        output = jnp.dot(mixed_ref[rows, :], wo_ref[...], preferred_element_type=F32)
        residual = emb_ref[CTX + rows.start : CTX + rows.stop, :].astype(F32)
        out_ref[rows, :] = (output + residual).astype(BF16)
        sent.append(pltpu.make_async_copy(out_ref.at[rows, :], out_hbm.at[rows, :], out_sems.at[t]))
        sent[-1].start()
    for copy in sent:
        copy.wait()


VMEM = pl.BlockSpec(memory_space=pltpu.VMEM)
SMEM = pl.BlockSpec(memory_space=pltpu.SMEM)
HBM = pl.BlockSpec(memory_space=pltpu.HBM)
MIB = 1024 * 1024
EARLY_MIB = 63
LAYER_MIB = 63


def held(array, columns=None):
    shape = array.shape if columns is None else (array.shape[0], columns)
    return pltpu.VMEM(shape, array.dtype)


def conv_scratch(count):
    return [
        pltpu.VMEM((2, count, 256), BF16),
        pltpu.VMEM((count, CH), F32),
        pltpu.VMEM((2, 3, MEL + 16, 2 * CH), F32),
        pltpu.VMEM((3 * 2 * CH, 2 * CH), BF16),
        pltpu.VMEM((2, count, 3 * 2 * CH), BF16),
        pltpu.VMEM((count, CH), F32),
    ]


def early_frames(me, chip, lens, own, k1, b1, k2, b2):
    count = EARLY + 128
    return pl.pallas_call(
        early_kernel,
        out_shape=jax.ShapeDtypeStruct((EARLY, PAIRS * CH), BF16),
        in_specs=[SMEM, VMEM] + [HBM] * 6,
        out_specs=HBM,
        scratch_shapes=[held(lens), held(own, count), held(k1), held(b1), held(k2), held(b2)]
        + [pltpu.SemaphoreType.DMA((6,))]
        + conv_scratch(count)
        + [pltpu.VMEM((EARLY, PAIRS * CH), BF16), pltpu.SemaphoreType.DMA((PAIRS // 2,))],
        compiler_params=pltpu.CompilerParams(vmem_limit_bytes=int(EARLY_MIB * MIB)),
        cost_estimate=pl.CostEstimate(flops=10 * 10**9, bytes_accessed=3 * 10**6, transcendentals=0),
        name="early_frames",
    )(me, chip, lens, own, k1, b1, k2, b2)


def layer(me, cross, chip, early, lens, own, k1, b1, k2, b2, gain, we, wh, wo):
    return pl.pallas_call(
        layer_kernel,
        out_shape=jax.ShapeDtypeStruct((SHARD, D), BF16),
        in_specs=[SMEM] + [VMEM] * 2 + [HBM] * 11,
        out_specs=HBM,
        scratch_shapes=[held(lens), held(own, LATE + 256)]
        + [held(array) for array in (k1, b1, k2, b2, gain, we, wh, wo)]
        + [pltpu.SemaphoreType.DMA((12,))]
        + conv_scratch(LATE + 384)
        + [
            pltpu.VMEM((WIN, PAIRS * CH), BF16),
            pltpu.VMEM((WIN, D), BF16),
            pltpu.VMEM((WIN, D), BF16),
            pltpu.VMEM((SHARD, D), BF16),
            pltpu.VMEM((WIN, D), BF16),
            pltpu.VMEM((D, WIN), BF16),
            pltpu.VMEM((KROWS, SHARD), F32),
            pltpu.VMEM((2, KROWS, 2 * QROWS), F32),
            pltpu.VMEM((2, 1, 2 * QROWS), F32),
            pltpu.VMEM((2, KROWS, 2 * QROWS), BF16),
            pltpu.VMEM((SHARD, D), BF16),
            pltpu.VMEM((SHARD, D), BF16),
            pltpu.SemaphoreType.DMA((2,)),
        ],
        compiler_params=pltpu.CompilerParams(vmem_limit_bytes=int(LAYER_MIB * MIB)),
        cost_estimate=pl.CostEstimate(flops=40 * 10**9, bytes_accessed=20 * 10**6, transcendentals=0),
        name="layer",
    )(me, cross, chip, early, lens, own, k1, b1, k2, b2, gain, we, wh, wo)


def cut_kernel(me_ref, own_hbm, cross_ref, chip_ref, sems):
    at = lax.rem(me_ref[0], 2) * (CAP - SHARD)
    other = (CAP - SHARD) - at
    copies = fetch(
        [own_hbm.at[:, pl.ds(pl.multiple_of(x, 128), SHARD)] for x in (at, other)],
        (cross_ref, chip_ref),
        sems,
    )
    for copy in copies:
        copy.wait()


def cut(me, own):
    part = jax.ShapeDtypeStruct((own.shape[0], SHARD), BF16)
    return pl.pallas_call(
        cut_kernel,
        out_shape=(part, part),
        in_specs=[SMEM, HBM],
        out_specs=(VMEM, VMEM),
        scratch_shapes=[pltpu.SemaphoreType.DMA((2,))],
        compiler_params=pltpu.CompilerParams(vmem_limit_bytes=4 * MIB),
        name="cut",
    )(me, own)


def on_device(log_mel, lengths, k1, b1, k2, b2, we, gain, wh, wo):
    devices = lax.axis_size(AXES)
    me = lax.axis_index(AXES).astype(jnp.int32).reshape(1)
    own = log_mel.T
    cross, chip = cut(me, own)
    ahead = [(i, i + 1) for i in range(0, devices, 2)]
    chip = lax.ppermute(chip, AXES, ahead + [(j, i) for i, j in ahead])
    ahead = [(i, i + 1) for i in range(1, devices - 1, 2)]
    cross = lax.ppermute(cross, AXES, ahead + [(j, i) for i, j in ahead])
    lens, b1, b2, gain = lengths.T, b1.reshape(1, -1), b2.reshape(1, -1), gain.reshape(1, -1)
    early = early_frames(me, chip, lens, own, k1, b1, k2, b2)
    return layer(me, cross, chip, early, lens, own, k1, b1, k2, b2, gain, we, wh, wo)


def solution(mesh):
    return jax.shard_map(
        on_device,
        mesh=mesh,
        in_specs=(P(AXES, None), P(), P(), P(), P(), P(), P(), P(), P(), P()),
        out_specs=P(AXES, None),
        check_vma=False,
    )
```

time: 53.5 us -> 44.9 us (0.84)
  the two profiles are of different devices: /device:TPU:23 before, /device:TPU:1 now
where the time goes in v2:
time: 44.9 us; the launch traced here: 44.7 us
  Pallas kernels  37.3 us (83%)
  starting transfers between devices  4.62 us (10%)
  local copies, waits for them, and re-layouts  2.53 us (6%)
    pallas_call x1, Pallas kernels, layer(): pl.pallas_call(layer_kernel, out_shape=jax.ShapeDtypeStruct((SHARD, D), B...  28.7 us
    pallas_call x1, Pallas kernels, early_frames(): pl.pallas_call(early_kernel, out_shape=jax.ShapeDtypeStruct((EARLY, PAIRS...  8.53 us
    ppermute x1, starting transfers between devices, on_device(): cross = lax.ppermute(cross, AXES, ahead + [(j, i) for i, j in ahead])  4.49 us
    unnamed x6, local copies, waits for them, and re-layouts  2.53 us
  transfers between devices with their start and end apart: 2, of which 0 were waited for; matrix products, arithmetic and copies ran while one was open for 0% of the time, Pallas kernels for 19%

profile of v2, /device:TPU:1, one launch (start us, length us, event | category | flops | bytes accessed | tf_op | source)
XLA Modules:
  0.0 44.7 jit_solution(2392378857834045415)
XLA Ops:
  0.0 0.0 copy-start
  0.0 1.1 %copy-done = bf16[896,320]{0,1:T(8,128)(2,1)S(1)} copy-done((bf16[896,320]{0,1:T(8,128)(2,1)S(1)}, bf16[896,320]{0,1:T(8,128)(2,1)}, u32[]{:S(2)}) %copy-start) | copy-done | bytes 573464
  1.1 0.1 cut.1
  1.1 0.1 collective-permute-start.1
  1.3 4.5 %collective-permute-start = (bf16[320,512]{1,0:T(8,128)(2,1)S(1)}, bf16[320,512]{1,0:T(8,128)(2,1)S(1)}, u32[]{:S(2)}, u32[]{:S(2)}) collective-permute-start(bf16[320,512]{1,0:T(8,128)(2,1)S(1)} %get-tuple-element.7), channel_id=1, source_target_pairs={{1,2},{3,4},{5,6},{7,8},{9,10},{11,12},{13,14},{15,16},{17,18},{19... | collective-permute-start | bytes 983048 | tf_op jit(solution)/shard_map/ppermute | solution.py:478
  5.8 0.0 collective-permute-done.1.chip_ref
  5.8 0.0 copy-start.1
  5.8 0.7 %copy-done.1 = bf16[320,512]{1,0:T(8,128)(2,1)} copy-done((bf16[320,512]{1,0:T(8,128)(2,1)}, bf16[320,512]{1,0:T(8,128)(2,1)S(1)}, u32[]{:S(2)}) %copy-start.1) | copy-done | bytes 327704
  6.5 8.5 %early_frames.1.early_hbm = bf16[384,2560]{1,0:T(8,128)(2,1)} custom-call(s32[1]{0:T(128)} %bitcast.me_ref, bf16[320,512]{1,0:T(8,128)(2,1)} %copy-done.1, s32[4,32]{1,0:T(4,128)} %bitcast.10, bf16[320,896]{1,0:T(8,128)(2,1)} %bitcast.6, bf16[9,128]{1,0:T(8,128)(2,1)} %k1_hbm.3, f32[1,128]{1,0:T(1,128)} %bitcast.12, bf16[1152,128]{1,0:T(8,128)(2,1)} %k2_hbm.3, ...), custom_call_target="tpu_custom_call" | custom-call | flops 10000000000 | bytes 3000000 | tf_op jit(solution)/shard_map/early_frames/pallas_call | solution.py:399
  15.0 0.0 collective-permute-done.cross_ref
  15.0 0.0 copy-start.2
  15.1 0.8 %copy-done.2 = bf16[320,512]{1,0:T(8,128)(2,1)} copy-done((bf16[320,512]{1,0:T(8,128)(2,1)}, bf16[320,512]{1,0:T(8,128)(2,1)S(1)}, u32[]{:S(2)}) %copy-start.2) | copy-done | bytes 327704
  15.8 28.7 %layer.1 = bf16[512,1024]{1,0:T(8,128)(2,1)} custom-call(s32[1]{0:T(128)} %bitcast.me_ref, bf16[320,512]{1,0:T(8,128)(2,1)} %copy-done.2, bf16[320,512]{1,0:T(8,128)(2,1)} %copy-done.1, bf16[384,2560]{1,0:T(8,128)(2,1)} %early_frames.1.early_hbm, s32[4,32]{1,0:T(4,128)} %bitcast.11, bf16[320,896]{1,0:T(8,128)(2,1)} %bitcast.7, bf16[9,128]{1,0:T(8,128)(2,1)} %k1_hbm.3, ...), custom_call_target="tpu_custom_call" | custom-call | flops 40000000000 | bytes 20000000 | tf_op jit(solution)/shard_map/layer/pallas_call | solution.py:415
Async XLA Ops:
  0.0 1.1 %copy-start = (bf16[896,320]{0,1:T(8,128)(2,1)S(1)}, bf16[896,320]{0,1:T(8,128)(2,1)}, u32[]{:S(2)}) copy-start(bf16[896,320]{0,1:T(8,128)(2,1)} %param.10) | copy-start | bytes 1720324
  1.1 4.6 %collective-permute-start.1 = (bf16[320,512]{1,0:T(8,128)(2,1)S(1)}, bf16[320,512]{1,0:T(8,128)(2,1)S(1)}, u32[]{:S(2)}, u32[]{:S(2)}) collective-permute-start(bf16[320,512]{1,0:T(8,128)(2,1)S(1)} %get-tuple-element.8), channel_id=1, source_target_pairs={{0,1},{2,3},{4,5},{6,7},{8,9},{10,11},{12,13},{14,15},{16,17},{18,... | collective-permute-start | bytes 983048 | tf_op jit(solution)/shard_map/ppermute | solution.py:476
  1.3 13.8 %collective-permute-start = (bf16[320,512]{1,0:T(8,128)(2,1)S(1)}, bf16[320,512]{1,0:T(8,128)(2,1)S(1)}, u32[]{:S(2)}, u32[]{:S(2)}) collective-permute-start(bf16[320,512]{1,0:T(8,128)(2,1)S(1)} %get-tuple-element.7), channel_id=1, source_target_pairs={{1,2},{3,4},{5,6},{7,8},{9,10},{11,12},{13,14},{15,16},{17,18},{19... | collective-permute-start | bytes 983048 | tf_op jit(solution)/shard_map/ppermute | solution.py:478
  5.8 0.7 %copy-start.1 = (bf16[320,512]{1,0:T(8,128)(2,1)}, bf16[320,512]{1,0:T(8,128)(2,1)S(1)}, u32[]{:S(2)}) copy-start(bf16[320,512]{1,0:T(8,128)(2,1)S(1)} %collective-permute-done.1.chip_ref) | copy-start | bytes 983044
  15.0 0.8 %copy-start.2 = (bf16[320,512]{1,0:T(8,128)(2,1)}, bf16[320,512]{1,0:T(8,128)(2,1)S(1)}, u32[]{:S(2)}) copy-start(bf16[320,512]{1,0:T(8,128)(2,1)S(1)} %collective-permute-done.cross_ref) | copy-start | bytes 983044

commit v3 on v2

--- a/solution.py
+++ b/solution.py
@@ -25,6 +25,7 @@
 QROWS = 128
 KROWS = 512
 AXES = ("seq", "inner")
+LOG2E = 1.4426950408889634
 F32 = jnp.float32
 BF16 = jnp.bfloat16
 
@@ -185,26 +186,26 @@
 
 
 def early_kernel(
-    me_ref, chip_ref, len_hbm, own_hbm, k1_hbm, b1_hbm, k2_hbm, b2_hbm, out_hbm,
-    len_ref, own_ref, k1_ref, b1_ref, k2_ref, b2_ref, sems,
+    me_ref, chip_hbm, len_hbm, own_hbm, k1_hbm, b1_hbm, k2_hbm, b2_hbm, out_hbm,
+    len_ref, own_ref, chip_ref, k1_ref, b1_ref, k2_ref, b2_ref, sems,
     x_ref, joined_ref, w1_ref, w2_ref, h_ref, low_ref, sec_ref, out_sems,
 ):
     me = me_ref[0]
     first = early_rows(me) - 128
     copies = fetch(
         (len_hbm, own_hbm.at[:, pl.ds(pl.multiple_of(first - 128, 128), EARLY + 128)])
-        + (k1_hbm, b1_hbm, k2_hbm, b2_hbm),
-        (len_ref, own_ref, k1_ref, b1_ref, k2_ref, b2_ref),
+        + (chip_hbm, k1_hbm, b1_hbm, k2_hbm, b2_hbm),
+        (len_ref, own_ref, chip_ref, k1_ref, b1_ref, k2_ref, b2_ref),
         sems,
     )
     copies[0].wait()
     frame, begin, _, own_low, own_high = frame_facts(me, len_ref, first, EARLY + 128)
+    for copy in copies[1:]:
+        copy.wait()
     chip = chip_ref[...].astype(F32)
     edge = jnp.where(lax.rem(me, 2) == 1, chip[:, 384:], chip[:, :128])
     other = jnp.concatenate([chip[:, 128:384], edge, chip[:, 128:256]], axis=1)
     owned = (frame >= own_low) & (frame < own_high)
-    for copy in copies[1:]:
-        copy.wait()
     raw = jnp.where(owned, own_ref[...].astype(F32), other)
     frame_taps(raw, begin == frame, x_ref, joined_ref)
     sent = []
@@ -223,10 +224,10 @@
 
 
 def layer_kernel(
-    me_ref, cross_ref, chip_ref, early_hbm, len_hbm, own_hbm, k1_hbm, b1_hbm, k2_hbm, b2_hbm, gain_hbm,
+    me_ref, cross_hbm, chip_hbm, early_hbm, len_hbm, own_hbm, k1_hbm, b1_hbm, k2_hbm, b2_hbm, gain_hbm,
     we_hbm, wh_hbm, wo_hbm, out_hbm,
-    len_ref, own_ref, k1_ref, b1_ref, k2_ref, b2_ref, gain_ref,
-    we_ref, wh_ref, wo_ref, sems,
+    len_ref, own_ref, chip_ref, cross_ref, k1_ref, b1_ref, k2_ref, b2_ref, gain_ref,
+    we_ref, wh_ref, wo_ref, sems, weight_sems,
     x_ref, joined_ref, w1_ref, w2_ref, h_ref, low_ref, sec_ref, emb_ref, norm_ref,
     q_ref, k_ref, vt_ref, mask_ref, score_ref, peak_ref, prob_ref, mixed_ref, out_ref, out_sems,
 ):
@@ -236,23 +237,28 @@
     late_own = pl.multiple_of(late - 256, 128)
     early = pl.multiple_of(early_rows(me), 128)
     copies = fetch(
-        (len_hbm, own_hbm.at[:, :128], own_hbm.at[:, pl.ds(late_own, LATE + 128)])
-        + (k1_hbm, b1_hbm, k2_hbm, b2_hbm, gain_hbm, we_hbm, early_hbm, wh_hbm, wo_hbm),
-        (len_ref, own_ref.at[:, :128], own_ref.at[:, 128:])
-        + (k1_ref, b1_ref, k2_ref, b2_ref, gain_ref, we_ref, sec_ref.at[pl.ds(early, EARLY), :], wh_ref, wo_ref),
+        (len_hbm, own_hbm.at[:, :128], own_hbm.at[:, pl.ds(late_own, LATE + 128)], chip_hbm.at[:, :256])
+        + (cross_hbm, k1_hbm, b1_hbm, k2_hbm, b2_hbm, gain_hbm),
+        (len_ref, own_ref.at[:, :128], own_ref.at[:, 128:], chip_ref, cross_ref)
+        + (k1_ref, b1_ref, k2_ref, b2_ref, gain_ref),
         sems,
     )
-    for copy in copies[:8]:
+    copies[0].wait()
+    frame, begin, _, own_low, _ = frame_facts(me, len_ref, 0, 256)
+    late_frame, late_begin, _, own_low, own_high = frame_facts(me, len_ref, late - 128, LATE + 128)
+    for copy in copies[1:]:
         copy.wait()
-    copies = copies[8:]
-    frame, begin, _, own_low, _ = frame_facts(me, len_ref, 0, 256)
+    copies = fetch(
+        (we_hbm, early_hbm, wh_hbm, wo_hbm),
+        (we_ref, sec_ref.at[pl.ds(early, EARLY), :], wh_ref, wo_ref),
+        weight_sems,
+    )
     cross = cross_ref[...].astype(F32)
-    up = jnp.where(odd, chip_ref[:, :256].astype(F32), cross[:, :256])
+    up = jnp.where(odd, chip_ref[...].astype(F32), cross[:, :256])
     raw = jnp.concatenate(
         [up[:, :128], jnp.where(frame[:, 128:] >= own_low, own_ref[:, :128].astype(F32), up[:, 128:])],
         axis=1,
     )
-    late_frame, late_begin, _, own_low, own_high = frame_facts(me, len_ref, late - 128, LATE + 128)
     other = jnp.where(odd, jnp.concatenate([cross[:, :128], cross[:, :256]], axis=1), cross[:, 128:])
     owned = (late_frame >= own_low) & (late_frame < own_high)
     raw = jnp.concatenate([raw, jnp.where(owned, own_ref[:, 128:].astype(F32), other)], axis=1)
@@ -266,22 +272,44 @@
     copies[0].wait()
     copies[1].wait()
     gain = gain_ref[...]
-    for t in range(WIN // ROWS):
-        rows = slice(t * ROWS, (t + 1) * ROWS)
-        emb = jnp.dot(sec_ref[rows, :], we_ref[...], preferred_element_type=F32).astype(BF16)
-        emb_ref[rows, :] = emb
-        values = emb.astype(F32)
+
+    def embed(rows, cols):
+        emb = jnp.dot(sec_ref[rows, :], we_ref[:, cols], preferred_element_type=F32)
+        emb_ref[rows, cols] = emb.astype(BF16)
+
+    def normalise(rows):
+        values = emb_ref[rows, :].astype(F32)
         center = values - jnp.mean(values, axis=1, keepdims=True)
         spread = jnp.mean(center * center, axis=1, keepdims=True)
         norm_ref[rows, :] = (center * lax.rsqrt(spread + 1e-05) * gain).astype(BF16)
 
+    def make_keys(rows, cols):
+        k = jnp.dot(
+            norm_ref[rows, :], wh_ref[:, D + cols.start : D + cols.stop], preferred_element_type=F32
+        )
+        k_ref[rows, cols] = k.astype(BF16)
+
+    blocks = [slice(n * 256, (n + 1) * 256) for n in range(D // 256)]
+    upper, lower = slice(0, ROWS), slice(ROWS, WIN)
+    quarter = ROWS // len(blocks)
+    for cols in blocks:
+        embed(upper, cols)
+    for n, cols in enumerate(blocks):
+        embed(lower, cols)
+        normalise(slice(n * quarter, (n + 1) * quarter))
     copies[2].wait()
+    for n, cols in enumerate(blocks):
+        make_keys(upper, cols)
+        normalise(slice(ROWS + n * quarter, ROWS + (n + 1) * quarter))
+    make_keys(lower, slice(0, D))
     q = jnp.dot(norm_ref[CTX : CTX + SHARD, :], wh_ref[:, :D], preferred_element_type=F32)
-    q_ref[...] = q.astype(BF16) * (HEAD**-0.5)
-    for t in range(WIN // ROWS):
-        rows = slice(t * ROWS, (t + 1) * ROWS)
-        k = jnp.dot(norm_ref[rows, :], wh_ref[:, D : 2 * D], preferred_element_type=F32)
-        k_ref[rows, :] = k.astype(BF16)
+    q = q.astype(BF16).astype(F32) * (HEAD**-0.5 * LOG2E)
+    q_high = q.astype(BF16)
+    q_low = (q - q_high.astype(F32)).astype(BF16)
+    for pair in range(HEADS // 2):
+        cols = slice(pair * 2 * HEAD, (pair + 1) * 2 * HEAD)
+        q_ref[:, pair * 4 * HEAD : pair * 4 * HEAD + 2 * HEAD] = q_high[:, cols]
+        q_ref[:, pair * 4 * HEAD + 2 * HEAD : (pair + 1) * 4 * HEAD] = q_low[:, cols]
     for t in range(WIN // 128):
         rows = slice(t * 128, (t + 1) * 128)
         v = jnp.dot(norm_ref[rows, :], wh_ref[:, 2 * D :], preferred_element_type=F32)
@@ -298,7 +326,7 @@
         seen = (key >= key_low[:, cols]) & (key < key_high[:, cols])
         mask_ref[:, cols] = jnp.where(seen, 0.0, -jnp.inf)
 
-    lane = iota((QROWS, 2 * HEAD), 1)
+    lane = lax.rem(iota((QROWS, 4 * HEAD), 1), 2 * HEAD)
     pairs = HEADS // 2
     steps = (SHARD // QROWS) * pairs
     summing = jnp.ones((16, KROWS), BF16)
@@ -310,12 +338,13 @@
 
     def score(slot, step):
         q_at, col = places(step)
-        qs = q_ref[pl.ds(q_at, QROWS), pl.ds(col, 2 * HEAD)]
+        qs = q_ref[pl.ds(q_at, QROWS), pl.ds(2 * col, 4 * HEAD)]
         zero = jnp.zeros_like(qs)
         both = jnp.concatenate(
             [jnp.where(lane < HEAD, qs, zero), jnp.where(lane >= HEAD, qs, zero)], axis=0
         )
         keys = k_ref[pl.ds(q_at, KROWS), pl.ds(col, 2 * HEAD)]
+        keys = jnp.concatenate([keys, keys], axis=1)
         scores = lax.dot_general(keys, both, (((1,), (1,)), ((), ())), preferred_element_type=F32)
         mask = mask_ref[:, pl.ds(q_at, QROWS)]
         scores = scores + jnp.concatenate([mask, mask], axis=1)
@@ -323,7 +352,7 @@
         peak_ref[slot] = jnp.max(scores, axis=0, keepdims=True)
 
     def weigh(slot):
-        prob_ref[slot] = jnp.exp(score_ref[slot] - peak_ref[slot]).astype(BF16)
+        prob_ref[slot] = jnp.exp2(score_ref[slot] - peak_ref[slot]).astype(BF16)
 
     def mix(slot, step):
         q_at, col = places(step)
@@ -348,24 +377,32 @@
         weigh(slot)
     for slot in range(2):
         score(slot, 2 + slot)
+    sent = []
+
+    def project(rows, cols):
+        output = jnp.dot(mixed_ref[rows, :], wo_ref[:, cols], preferred_element_type=F32)
+        residual = emb_ref[CTX + rows.start : CTX + rows.stop, cols].astype(F32)
+        out_ref[rows, cols] = (output + residual).astype(BF16)
+
+    def send(rows):
+        sent.append(pltpu.make_async_copy(out_ref.at[rows, :], out_hbm.at[rows, :], out_sems.at[len(sent)]))
+        sent[-1].start()
+
+    copies[3].wait()
+    halves = slice(0, SHARD // 2), slice(SHARD // 2, SHARD)
     for it in range(steps // 2 - 2):
         attend_two(it)
+        if steps // 4 <= it < steps // 4 + len(blocks):
+            project(halves[0], blocks[it - steps // 4])
+    send(halves[0])
     for slot in range(2):
         mix(slot, steps - 4 + slot)
     for slot in range(2):
         weigh(slot)
     for slot in range(2):
         mix(slot, steps - 2 + slot)
-
-    copies[3].wait()
-    sent = []
-    for t in range(2):
-        rows = slice(t * SHARD // 2, (t + 1) * SHARD // 2)
-        output = jnp.dot(mixed_ref[rows, :], wo_ref[...], preferred_element_type=F32)
-        residual = emb_ref[CTX + rows.start : CTX + rows.stop, :].astype(F32)
-        out_ref[rows, :] = (output + residual).astype(BF16)
-        sent.append(pltpu.make_async_copy(out_ref.at[rows, :], out_hbm.at[rows, :], out_sems.at[t]))
-        sent[-1].start()
+    project(halves[1], slice(0, D))
+    send(halves[1])
     for copy in sent:
         copy.wait()
 
@@ -399,10 +436,10 @@
     return pl.pallas_call(
         early_kernel,
         out_shape=jax.ShapeDtypeStruct((EARLY, PAIRS * CH), BF16),
-        in_specs=[SMEM, VMEM] + [HBM] * 6,
+        in_specs=[SMEM] + [HBM] * 7,
         out_specs=HBM,
-        scratch_shapes=[held(lens), held(own, count), held(k1), held(b1), held(k2), held(b2)]
-        + [pltpu.SemaphoreType.DMA((6,))]
+        scratch_shapes=[held(lens), held(own, count), held(chip), held(k1), held(b1), held(k2), held(b2)]
+        + [pltpu.SemaphoreType.DMA((7,))]
         + conv_scratch(count)
         + [pltpu.VMEM((EARLY, PAIRS * CH), BF16), pltpu.SemaphoreType.DMA((PAIRS // 2,))],
         compiler_params=pltpu.CompilerParams(vmem_limit_bytes=int(EARLY_MIB * MIB)),
@@ -415,17 +452,17 @@
     return pl.pallas_call(
         layer_kernel,
         out_shape=jax.ShapeDtypeStruct((SHARD, D), BF16),
-        in_specs=[SMEM] + [VMEM] * 2 + [HBM] * 11,
+        in_specs=[SMEM] + [HBM] * 13,
         out_specs=HBM,
-        scratch_shapes=[held(lens), held(own, LATE + 256)]
+        scratch_shapes=[held(lens), held(own, LATE + 256), held(chip, 256), held(cross)]
         + [held(array) for array in (k1, b1, k2, b2, gain, we, wh, wo)]
-        + [pltpu.SemaphoreType.DMA((12,))]
+        + [pltpu.SemaphoreType.DMA((10,)), pltpu.SemaphoreType.DMA((4,))]
         + conv_scratch(LATE + 384)
         + [
             pltpu.VMEM((WIN, PAIRS * CH), BF16),
             pltpu.VMEM((WIN, D), BF16),
             pltpu.VMEM((WIN, D), BF16),
-            pltpu.VMEM((SHARD, D), BF16),
+            pltpu.VMEM((SHARD, 2 * D), BF16),
             pltpu.VMEM((WIN, D), BF16),
             pltpu.VMEM((D, WIN), BF16),
             pltpu.VMEM((KROWS, SHARD), F32),

time: 44.9 us -> 42.7 us (0.951)
  Pallas kernels: 37.3 us -> 35.1 us
    pallas_call x1, Pallas kernels: 28.7 us -> 27.4 us  [layer(): pl.pallas_call(layer_kernel, out_shape=jax.ShapeDtypeStruct((SHARD, D), B...]
    pallas_call x1, Pallas kernels: 8.53 us -> 7.66 us  [early_frames(): pl.pallas_call(early_kernel, out_shape=jax.ShapeDtypeStruct((EARLY, PAIRS...]
  transfers between devices with their start and end apart: 2 -> 2, of which waited for: 0 -> 0; matrix products, arithmetic and copies ran while one was open for 0% -> 0% of each run, Pallas kernels for 19% -> 18%
where the time goes in v3:
time: 42.7 us; the launch traced here: 42.5 us
  Pallas kernels  35.1 us (82%)
  starting transfers between devices  4.62 us (11%)
  local copies, waits for them, and re-layouts  2.53 us (6%)
    pallas_call x1, Pallas kernels, layer(): pl.pallas_call(layer_kernel, out_shape=jax.ShapeDtypeStruct((SHARD, D), B...  27.4 us
    pallas_call x1, Pallas kernels, early_frames(): pl.pallas_call(early_kernel, out_shape=jax.ShapeDtypeStruct((EARLY, PAIRS...  7.66 us
    ppermute x1, starting transfers between devices, on_device(): cross = lax.ppermute(cross, AXES, ahead + [(j, i) for i, j in ahead])  4.49 us
    unnamed x6, local copies, waits for them, and re-layouts  2.53 us
  transfers between devices with their start and end apart: 2, of which 0 were waited for; matrix products, arithmetic and copies ran while one was open for 0% of the time, Pallas kernels for 18%

profile of v3, /device:TPU:1, one launch (start us, length us, event | category | flops | bytes accessed | tf_op | source)
XLA Modules:
  0.0 42.5 jit_solution(15167471340466519585)
XLA Ops:
  0.0 0.0 copy-start
  0.0 1.1 %copy-done = bf16[896,320]{0,1:T(8,128)(2,1)S(1)} copy-done((bf16[896,320]{0,1:T(8,128)(2,1)S(1)}, bf16[896,320]{0,1:T(8,128)(2,1)}, u32[]{:S(2)}) %copy-start) | copy-done | bytes 573464
  1.1 0.1 cut.1
  1.1 0.1 collective-permute-start.1
  1.3 4.5 %collective-permute-start = (bf16[320,512]{1,0:T(8,128)(2,1)S(1)}, bf16[320,512]{1,0:T(8,128)(2,1)S(1)}, u32[]{:S(2)}, u32[]{:S(2)}) collective-permute-start(bf16[320,512]{1,0:T(8,128)(2,1)S(1)} %get-tuple-element.7), channel_id=1, source_target_pairs={{1,2},{3,4},{5,6},{7,8},{9,10},{11,12},{13,14},{15,16},{17,18},{19... | collective-permute-start | bytes 983048 | tf_op jit(solution)/shard_map/ppermute | solution.py:515
  5.8 0.0 collective-permute-done.1.chip_hbm
  5.8 0.0 copy-start.1
  5.8 0.7 %copy-done.1 = bf16[320,512]{1,0:T(8,128)(2,1)} copy-done((bf16[320,512]{1,0:T(8,128)(2,1)}, bf16[320,512]{1,0:T(8,128)(2,1)S(1)}, u32[]{:S(2)}) %copy-start.1) | copy-done | bytes 327704
  6.5 7.7 %early_frames.1.early_hbm = bf16[384,2560]{1,0:T(8,128)(2,1)} custom-call(s32[1]{0:T(128)} %bitcast.me_ref, bf16[320,512]{1,0:T(8,128)(2,1)} %copy-done.1, s32[4,32]{1,0:T(4,128)} %bitcast.10, bf16[320,896]{1,0:T(8,128)(2,1)} %bitcast.6, bf16[9,128]{1,0:T(8,128)(2,1)} %k1_hbm.3, f32[1,128]{1,0:T(1,128)} %bitcast.12, bf16[1152,128]{1,0:T(8,128)(2,1)} %k2_hbm.3, ...), custom_call_target="tpu_custom_call" | custom-call | flops 10000000000 | bytes 3000000 | tf_op jit(solution)/shard_map/early_frames/pallas_call | solution.py:436
  14.2 0.0 collective-permute-done.cross_hbm
  14.2 0.0 copy-start.2
  14.2 0.8 %copy-done.2 = bf16[320,512]{1,0:T(8,128)(2,1)} copy-done((bf16[320,512]{1,0:T(8,128)(2,1)}, bf16[320,512]{1,0:T(8,128)(2,1)S(1)}, u32[]{:S(2)}) %copy-start.2) | copy-done | bytes 327704
  14.9 27.4 %layer.1 = bf16[512,1024]{1,0:T(8,128)(2,1)} custom-call(s32[1]{0:T(128)} %bitcast.me_ref, bf16[320,512]{1,0:T(8,128)(2,1)} %copy-done.2, bf16[320,512]{1,0:T(8,128)(2,1)} %copy-done.1, bf16[384,2560]{1,0:T(8,128)(2,1)} %early_frames.1.early_hbm, s32[4,32]{1,0:T(4,128)} %bitcast.11, bf16[320,896]{1,0:T(8,128)(2,1)} %bitcast.7, bf16[9,128]{1,0:T(8,128)(2,1)} %k1_hbm.3, ...), custom_call_target="tpu_custom_call" | custom-call | flops 40000000000 | bytes 20000000 | tf_op jit(solution)/shard_map/layer/pallas_call | solution.py:452
Async XLA Ops:
  0.0 1.1 %copy-start = (bf16[896,320]{0,1:T(8,128)(2,1)S(1)}, bf16[896,320]{0,1:T(8,128)(2,1)}, u32[]{:S(2)}) copy-start(bf16[896,320]{0,1:T(8,128)(2,1)} %param.10) | copy-start | bytes 1720324
  1.1 4.6 %collective-permute-start.1 = (bf16[320,512]{1,0:T(8,128)(2,1)S(1)}, bf16[320,512]{1,0:T(8,128)(2,1)S(1)}, u32[]{:S(2)}, u32[]{:S(2)}) collective-permute-start(bf16[320,512]{1,0:T(8,128)(2,1)S(1)} %get-tuple-element.8), channel_id=1, source_target_pairs={{0,1},{2,3},{4,5},{6,7},{8,9},{10,11},{12,13},{14,15},{16,17},{18,... | collective-permute-start | bytes 983048 | tf_op jit(solution)/shard_map/ppermute | solution.py:513
  1.3 12.9 %collective-permute-start = (bf16[320,512]{1,0:T(8,128)(2,1)S(1)}, bf16[320,512]{1,0:T(8,128)(2,1)S(1)}, u32[]{:S(2)}, u32[]{:S(2)}) collective-permute-start(bf16[320,512]{1,0:T(8,128)(2,1)S(1)} %get-tuple-element.7), channel_id=1, source_target_pairs={{1,2},{3,4},{5,6},{7,8},{9,10},{11,12},{13,14},{15,16},{17,18},{19... | collective-permute-start | bytes 983048 | tf_op jit(solution)/shard_map/ppermute | solution.py:515
  5.8 0.7 %copy-start.1 = (bf16[320,512]{1,0:T(8,128)(2,1)}, bf16[320,512]{1,0:T(8,128)(2,1)S(1)}, u32[]{:S(2)}) copy-start(bf16[320,512]{1,0:T(8,128)(2,1)S(1)} %collective-permute-done.1.chip_hbm) | copy-start | bytes 983044
  14.2 0.8 %copy-start.2 = (bf16[320,512]{1,0:T(8,128)(2,1)}, bf16[320,512]{1,0:T(8,128)(2,1)S(1)}, u32[]{:S(2)}) copy-start(bf16[320,512]{1,0:T(8,128)(2,1)S(1)} %collective-permute-done.cross_hbm) | copy-start | bytes 983044

commit v4 on v3

--- a/solution.py
+++ b/solution.py
@@ -411,7 +411,7 @@
 SMEM = pl.BlockSpec(memory_space=pltpu.SMEM)
 HBM = pl.BlockSpec(memory_space=pltpu.HBM)
 MIB = 1024 * 1024
-EARLY_MIB = 63
+EARLY_MIB = 58
 LAYER_MIB = 63
 
 

time: 42.7 us -> 42.7 us (level)
  no operation moved by 1% of the time
where the time goes in v4:
time: 42.7 us; the launch traced here: 42.5 us
  Pallas kernels  35.1 us (82%)
  starting transfers between devices  4.62 us (11%)
  local copies, waits for them, and re-layouts  2.53 us (6%)
    pallas_call x1, Pallas kernels, layer(): pl.pallas_call(layer_kernel, out_shape=jax.ShapeDtypeStruct((SHARD, D), B...  27.4 us
    pallas_call x1, Pallas kernels, early_frames(): pl.pallas_call(early_kernel, out_shape=jax.ShapeDtypeStruct((EARLY, PAIRS...  7.66 us
    ppermute x1, starting transfers between devices, on_device(): cross = lax.ppermute(cross, AXES, ahead + [(j, i) for i, j in ahead])  4.49 us
    unnamed x6, local copies, waits for them, and re-layouts  2.53 us
  transfers between devices with their start and end apart: 2, of which 0 were waited for; matrix products, arithmetic and copies ran while one was open for 0% of the time, Pallas kernels for 18%

profile of v4, /device:TPU:1, one launch (start us, length us, event | category | flops | bytes accessed | tf_op | source)
XLA Modules:
  0.0 42.5 jit_solution(419681714663582733)
XLA Ops:
  0.0 0.0 copy-start
  0.0 1.1 %copy-done = bf16[896,320]{0,1:T(8,128)(2,1)S(1)} copy-done((bf16[896,320]{0,1:T(8,128)(2,1)S(1)}, bf16[896,320]{0,1:T(8,128)(2,1)}, u32[]{:S(2)}) %copy-start) | copy-done | bytes 573464
  1.1 0.1 cut.1
  1.1 0.1 collective-permute-start.1
  1.3 4.5 %collective-permute-start = (bf16[320,512]{1,0:T(8,128)(2,1)S(1)}, bf16[320,512]{1,0:T(8,128)(2,1)S(1)}, u32[]{:S(2)}, u32[]{:S(2)}) collective-permute-start(bf16[320,512]{1,0:T(8,128)(2,1)S(1)} %get-tuple-element.7), channel_id=1, source_target_pairs={{1,2},{3,4},{5,6},{7,8},{9,10},{11,12},{13,14},{15,16},{17,18},{19... | collective-permute-start | bytes 983048 | tf_op jit(solution)/shard_map/ppermute | solution.py:515
  5.8 0.0 collective-permute-done.1.chip_hbm
  5.8 0.0 copy-start.1
  5.8 0.7 %copy-done.1 = bf16[320,512]{1,0:T(8,128)(2,1)} copy-done((bf16[320,512]{1,0:T(8,128)(2,1)}, bf16[320,512]{1,0:T(8,128)(2,1)S(1)}, u32[]{:S(2)}) %copy-start.1) | copy-done | bytes 327704
  6.5 7.7 %early_frames.1.early_hbm = bf16[384,2560]{1,0:T(8,128)(2,1)} custom-call(s32[1]{0:T(128)} %bitcast.me_ref, bf16[320,512]{1,0:T(8,128)(2,1)} %copy-done.1, s32[4,32]{1,0:T(4,128)} %bitcast.10, bf16[320,896]{1,0:T(8,128)(2,1)} %bitcast.6, bf16[9,128]{1,0:T(8,128)(2,1)} %k1_hbm.3, f32[1,128]{1,0:T(1,128)} %bitcast.12, bf16[1152,128]{1,0:T(8,128)(2,1)} %k2_hbm.3, ...), custom_call_target="tpu_custom_call" | custom-call | flops 10000000000 | bytes 3000000 | tf_op jit(solution)/shard_map/early_frames/pallas_call | solution.py:436
  14.2 0.0 collective-permute-done.cross_hbm
  14.2 0.0 copy-start.2
  14.2 0.8 %copy-done.2 = bf16[320,512]{1,0:T(8,128)(2,1)} copy-done((bf16[320,512]{1,0:T(8,128)(2,1)}, bf16[320,512]{1,0:T(8,128)(2,1)S(1)}, u32[]{:S(2)}) %copy-start.2) | copy-done | bytes 327704
  14.9 27.4 %layer.1 = bf16[512,1024]{1,0:T(8,128)(2,1)} custom-call(s32[1]{0:T(128)} %bitcast.me_ref, bf16[320,512]{1,0:T(8,128)(2,1)} %copy-done.2, bf16[320,512]{1,0:T(8,128)(2,1)} %copy-done.1, bf16[384,2560]{1,0:T(8,128)(2,1)} %early_frames.1.early_hbm, s32[4,32]{1,0:T(4,128)} %bitcast.11, bf16[320,896]{1,0:T(8,128)(2,1)} %bitcast.7, bf16[9,128]{1,0:T(8,128)(2,1)} %k1_hbm.3, ...), custom_call_target="tpu_custom_call" | custom-call | flops 40000000000 | bytes 20000000 | tf_op jit(solution)/shard_map/layer/pallas_call | solution.py:452
Async XLA Ops:
  0.0 1.1 %copy-start = (bf16[896,320]{0,1:T(8,128)(2,1)S(1)}, bf16[896,320]{0,1:T(8,128)(2,1)}, u32[]{:S(2)}) copy-start(bf16[896,320]{0,1:T(8,128)(2,1)} %param.10) | copy-start | bytes 1720324
  1.1 4.6 %collective-permute-start.1 = (bf16[320,512]{1,0:T(8,128)(2,1)S(1)}, bf16[320,512]{1,0:T(8,128)(2,1)S(1)}, u32[]{:S(2)}, u32[]{:S(2)}) collective-permute-start(bf16[320,512]{1,0:T(8,128)(2,1)S(1)} %get-tuple-element.8), channel_id=1, source_target_pairs={{0,1},{2,3},{4,5},{6,7},{8,9},{10,11},{12,13},{14,15},{16,17},{18,... | collective-permute-start | bytes 983048 | tf_op jit(solution)/shard_map/ppermute | solution.py:513
  1.3 12.9 %collective-permute-start = (bf16[320,512]{1,0:T(8,128)(2,1)S(1)}, bf16[320,512]{1,0:T(8,128)(2,1)S(1)}, u32[]{:S(2)}, u32[]{:S(2)}) collective-permute-start(bf16[320,512]{1,0:T(8,128)(2,1)S(1)} %get-tuple-element.7), channel_id=1, source_target_pairs={{1,2},{3,4},{5,6},{7,8},{9,10},{11,12},{13,14},{15,16},{17,18},{19... | collective-permute-start | bytes 983048 | tf_op jit(solution)/shard_map/ppermute | solution.py:515
  5.8 0.7 %copy-start.1 = (bf16[320,512]{1,0:T(8,128)(2,1)}, bf16[320,512]{1,0:T(8,128)(2,1)S(1)}, u32[]{:S(2)}) copy-start(bf16[320,512]{1,0:T(8,128)(2,1)S(1)} %collective-permute-done.1.chip_hbm) | copy-start | bytes 983044
  14.2 0.8 %copy-start.2 = (bf16[320,512]{1,0:T(8,128)(2,1)}, bf16[320,512]{1,0:T(8,128)(2,1)S(1)}, u32[]{:S(2)}) copy-start(bf16[320,512]{1,0:T(8,128)(2,1)S(1)} %collective-permute-done.cross_hbm) | copy-start | bytes 983044
